TPU v7x, 32 devices: a whole 2x2x4 slice. The times are simulated.
32 devices in a mesh: dp: 4 (over x, core), seq: 2 (over y), tensor: 4 (over z).
Axes of the slice: x: 2, y: 2, z: 4, core: 2. Of those that a mesh axis runs over, the one named last changes fastest.
Arguments:
- hidden: bfloat16 [1024, 28672], P(('dp', 'seq'), 'tensor'), may hold values from -6 to 6
- weight: bfloat16 [28672, 4096], P('tensor', 'seq'), may hold values from -0.03125 to 0.03125
- out_grad: bfloat16 [1024, 4096], P(('dp', 'tensor'), 'seq'), may hold values from -6 to 6
Outputs:
- output: bfloat16 [1024, 4096], P(('dp', 'tensor'), 'seq')
- grad_hidden: bfloat16 [1024, 28672], P(('dp', 'seq'), 'tensor')
- grad_weight: bfloat16 [28672, 4096], P('tensor', 'seq')
All inputs are finite; a program needn't handle non-finite values.
Results may differ from a plain program's by a relative error of at most 0.017.
Values may be sent and summed in bfloat16 or wider, within the bound.
No kernel may reach another device: no remote copies, remote signals or barrier semaphores. Data moves between devices by JAX's collectives and lax.ppermute only.
A program may use at most 192 MiB of HBM per device.

v0:
```python
import jax
import jax.numpy as jnp
from jax import lax
from jax.sharding import PartitionSpec as P

HB = 512


def partner_2(shard, axis, distance):
    return lax.ppermute(shard, axis, [(i, i ^ 1 << distance) for i in range(lax.axis_size(axis))])


def walsh_table(table_order):
    matrix = jnp.ones((1, 1), jnp.float32)
    while matrix.shape[0] < table_order:
        matrix = jnp.concatenate(
            [jnp.concatenate([matrix, matrix], 1), jnp.concatenate([matrix, -matrix], 1)], 0
        )
    return matrix


def local_blocks(values, inner_table):
    row_count, feature_count = values.shape
    block_size = inner_table.shape[0]
    shaped = values.reshape(row_count, feature_count // block_size, block_size)
    if values.dtype == jnp.bfloat16:
        mixed_rows = jnp.einsum(
            "rbk,kl->rbl",
            shaped,
            inner_table.astype(jnp.bfloat16),
            preferred_element_type=jnp.float32,
        )
    else:
        mixed_rows = jnp.einsum("rbk,kl->rbl", shaped, inner_table, precision=lax.Precision.HIGHEST)
    return mixed_rows.reshape(row_count, feature_count)


def butterfly(values):
    axis_count = lax.axis_size("tensor")
    device_index = lax.axis_index("tensor")
    for bit_index in range(axis_count.bit_length() - 1):
        partner = partner_2(values.astype(jnp.bfloat16), "tensor", bit_index).astype(values.dtype)
        upper_half = device_index // (1 << bit_index) % 2 == 1
        values = jnp.where(upper_half, partner - values, values + partner)
    return values


def rotate(values, inner_table, norm_scale):
    return (butterfly(local_blocks(values, inner_table)) * norm_scale).astype(jnp.bfloat16)


def body(hidden, weight, out_grad):
    inner_table = walsh_table(HB)
    norm_scale = 1.0 / float(lax.axis_size("tensor") * HB) ** 0.5
    rotated = rotate(hidden, inner_table, norm_scale)
    gathered = lax.all_gather(rotated, "seq", axis=0, tiled=True)
    partial_sums = jnp.dot(gathered, weight, preferred_element_type=jnp.float32)
    output = lax.psum_scatter(
        partial_sums.astype(jnp.bfloat16), "tensor", scatter_dimension=0, tiled=True
    )
    grads_all = lax.all_gather(out_grad, "tensor", axis=0, tiled=True)
    token_total = hidden.shape[0] * lax.axis_size("seq") * lax.axis_size("dp")
    grad_term = lax.dot_general(
        gathered, grads_all, (((0,), (0,)), ((), ())), preferred_element_type=jnp.float32
    )
    grad_weight = lax.psum(
        (grad_term * (1.0 / float(token_total) ** 0.5)).astype(jnp.bfloat16), "dp"
    )
    rotated_grad = lax.psum_scatter(
        lax.dot_general(
            grads_all, weight, (((1,), (1,)), ((), ())), preferred_element_type=jnp.float32
        ).astype(jnp.bfloat16),
        "seq",
        scatter_dimension=0,
        tiled=True,
    ).astype(jnp.float32)
    grad_hidden = rotate(rotated_grad, inner_table, norm_scale)
    return (output, grad_hidden, grad_weight)


def solution(mesh):
    in_specs = (P(("dp", "seq"), "tensor"), P("tensor", "seq"), P(("dp", "tensor"), "seq"))
    out_specs = (P(("dp", "tensor"), "seq"), P(("dp", "seq"), "tensor"), P("tensor", "seq"))
    return jax.shard_map(body, mesh=mesh, in_specs=in_specs, out_specs=out_specs, check_vma=False)
```

profile of v0, /device:TPU:0, one launch (start us, length us, event | category | flops | bytes accessed | tf_op | source)
XLA Modules:
  0.0 834.6 jit_solution(2826757487268747441)
XLA Ops:
  7.2 0.0 all-gather.5.cloned.1.call-start
  7.2 3.3 copy.11
  10.6 1.1 fusion.10
  11.7 1.8 copy-done
  13.5 1.4 bitcast_convert_fusion.1
  14.9 3.0 collective-permute-start
  18.0 40.2 %collective-permute-done = bf16[128,7168]{0,1:T(8,128)(2,1)S(1)} collective-permute-done((bf16[128,7168]{0,1:T(8,128)(2,1)}, bf16[128,7168]{0,1:T(8,128)(2,1)S(1)}, u32[]{:S(2)}, u32[]{:S(2)}) %collective-permute-start) | collective-permute-done | bytes 1835040 | tf_op jit(solution)/shard_map/ppermute | solution.py:10
  58.2 3.9 fusion.9
  62.1 2.8 collective-permute-start.1
  64.8 0.0 all-gather.3.cloned.1.call-start
  64.9 95.7 %collective-permute-done.1 = bf16[128,7168]{0,1:T(8,128)(2,1)} collective-permute-done((bf16[128,7168]{0,1:T(8,128)(2,1)}, bf16[128,7168]{0,1:T(8,128)(2,1)}, u32[]{:S(2)}, u32[]{:S(2)}) %collective-permute-start.1) | collective-permute-done | bytes 1835040 | tf_op jit(solution)/shard_map/ppermute | solution.py:10
  160.6 5.0 fusion.3
  165.7 0.0 reduce-scatter.5.cloned.1.call-start
  165.7 16.3 %convolution_convert_fusion = bf16[256,7168]{1,0:T(8,128)(2,1)} fusion(bf16[256,2048]{1,0:T(8,128)(2,1)} %all-gather.5.cloned.1.call-done, bf16[7168,2048]{1,0:T(8,128)(2,1)} %param.4), kind=kOutput, calls=%fused_computation.1 | convolution fusion | flops 7518027776 | bytes 34078720 | tf_op jit(solution)/shard_map/dot_general | solution.py:70
  182.1 0.0 reduce-scatter.3.cloned.1.call-start
  182.2 35.5 %all-gather.3.cloned.1.call-done = bf16[256,7168]{0,1:T(8,128)(2,1)} async-done(((bf16[128,7168]{0,1:T(8,128)(2,1)}), bf16[256,7168]{0,1:T(8,128)(2,1)}) %all-gather.3.cloned.1.call-update) | async-done | bytes 3670032 | tf_op jit(solution)/shard_map/all_gather | solution.py:56
  217.6 16.6 %convolution_convert_fusion.1 = bf16[256,2048]{1,0:T(8,128)(2,1)} fusion(bf16[256,7168]{0,1:T(8,128)(2,1)} %all-gather.3.cloned.1.call-done, bf16[7168,2048]{1,0:T(8,128)(2,1)} %param.4), kind=kOutput, calls=%fused_computation.20 | convolution fusion | flops 7516717056 | bytes 34078720 | tf_op jit(solution)/shard_map/dot_general | solution.py:57
  234.2 0.2 all-reduce.2.cloned.1.call-start
  234.5 14.7 %multiply_convert_fusion = bf16[7168,2048]{1,0:T(8,128)(2,1)} fusion(bf16[256,7168]{0,1:T(8,128)(2,1)} %all-gather.3.cloned.1.call-done, bf16[256,2048]{1,0:T(8,128)(2,1)S(1)} %copy-done.3), kind=kOutput, calls=%fused_computation | convolution fusion | flops 7545552896 | bytes 34078720 | tf_op jit(solution)/shard_map/dot_general | solution.py:63
  249.2 19.8 %reduce-scatter.5.cloned.1.call-done = bf16[128,7168]{1,0:T(8,128)(2,1)} async-done(((bf16[256,7168]{1,0:T(8,128)(2,1)}), bf16[128,7168]{1,0:T(8,128)(2,1)}) %reduce-scatter.5.cloned.1.call-update) | async-done | bytes 1835024 | tf_op jit(solution)/shard_map/reduce_scatter | solution.py:69
  269.0 3.3 copy.13
  272.3 3.3 fusion.11
  275.7 0.2 bitcast_convert_fusion
  275.9 1.5 collective-permute-start.2
  277.4 57.1 %collective-permute-done.2 = bf16[128,7168]{0,1:T(8,128)(2,1)S(1)} collective-permute-done((bf16[128,7168]{0,1:T(8,128)(2,1)S(1)}, bf16[128,7168]{0,1:T(8,128)(2,1)S(1)}, u32[]{:S(2)}, u32[]{:S(2)}) %collective-permute-start.2) | collective-permute-done | bytes 1835040 | tf_op jit(solution)/shard_map/ppermute | solution.py:10
  334.5 0.6 fusion.8
  335.1 2.5 collective-permute-start.3
  337.6 78.8 %collective-permute-done.3 = bf16[128,7168]{0,1:T(8,128)(2,1)S(1)} collective-permute-done((bf16[128,7168]{0,1:T(8,128)(2,1)S(1)}, bf16[128,7168]{0,1:T(8,128)(2,1)S(1)}, u32[]{:S(2)}, u32[]{:S(2)}) %collective-permute-start.3) | collective-permute-done | bytes 1835040 | tf_op jit(solution)/shard_map/ppermute | solution.py:10
  416.4 1.2 fusion.7
  417.6 2.9 copy.16
  420.5 387.5 %all-reduce.2.cloned.1.call-done = bf16[7168,2048]{1,0:T(8,128)(2,1)} async-done(((bf16[7168,2048]{1,0:T(8,128)(2,1)}), bf16[7168,2048]{1,0:T(8,128)(2,1)}) %all-reduce.2.cloned.1.call-update) | async-done | bytes 29360144 | tf_op jit(solution)/shard_map/psum | solution.py:66
  808.0 20.1 %copy.21 = bf16[7168,2048]{1,0:T(8,128)(2,1)} copy(bf16[7168,2048]{1,0:T(8,128)(2,1)} %all-reduce.2.cloned.1.call-done) | data formatting | bytes 58720256
  (14 shorter events, 0.1 us)
Async XLA Ops:
  7.2 3.4 copy-start.2
  7.2 158.6 %all-gather.5.cloned.1.call-start = ((), (), s32[]{:S(2)}) async-start(), calls=%async_computation.4 | async-start | bytes 1310720 | tf_op jit(solution)/shard_map/all_gather | solution.py:61
  11.7 1.8 copy-start
  14.9 43.2 %collective-permute-start = (bf16[128,7168]{0,1:T(8,128)(2,1)}, bf16[128,7168]{0,1:T(8,128)(2,1)S(1)}, u32[]{:S(2)}, u32[]{:S(2)}) collective-permute-start(bf16[128,7168]{0,1:T(8,128)(2,1)} %bitcast_convert_fusion.1), channel_id=1, source_target_pairs={{0,1},{1,0},{2,3},{3,2},{4,5},{5,4},{6,7},{7,6},{8,9},{9,8},{10,11... | collective-permute-start | bytes 5505032 | tf_op jit(solution)/shard_map/ppermute | solution.py:10
  62.1 98.6 %collective-permute-start.1 = (bf16[128,7168]{0,1:T(8,128)(2,1)}, bf16[128,7168]{0,1:T(8,128)(2,1)}, u32[]{:S(2)}, u32[]{:S(2)}) collective-permute-start(bf16[128,7168]{0,1:T(8,128)(2,1)} %fusion.9), channel_id=1, source_target_pairs={{0,2},{1,3},{2,0},{3,1},{4,6},{5,7},{6,4},{7,5},{8,10},{9,11},{10,... | collective-permute-start | bytes 5505032 | tf_op jit(solution)/shard_map/ppermute | solution.py:10
  64.8 152.8 %all-gather.3.cloned.1.call-start = ((), (), s32[]{:S(2)}) async-start(), calls=%async_computation.2 | async-start | bytes 5505024 | tf_op jit(solution)/shard_map/all_gather | solution.py:56
  165.7 103.3 %reduce-scatter.5.cloned.1.call-start = ((), (), s32[]{:S(2)}) async-start(), calls=%async_computation.5 | async-start | bytes 5505024 | tf_op jit(solution)/shard_map/reduce_scatter | solution.py:69
  182.1 52.4 %copy-start.3 = (bf16[256,2048]{1,0:T(8,128)(2,1)S(1)}, bf16[256,2048]{1,0:T(8,128)(2,1)}, u32[]{:S(2)}) copy-start(bf16[256,2048]{1,0:T(8,128)(2,1)} %all-gather.5.cloned.1.call-done) | copy-start | bytes 3145732
  182.1 238.3 %reduce-scatter.3.cloned.1.call-start = ((), (), s32[]{:S(2)}) async-start(), calls=%async_computation.3 | async-start | bytes 1310720 | tf_op jit(solution)/shard_map/reduce_scatter | solution.py:58
  234.2 573.8 %all-reduce.2.cloned.1.call-start = ((), (), s32[]{:S(2)}) async-start(), calls=%async_computation.6 | async-start | bytes 58720256 | tf_op jit(solution)/shard_map/psum | solution.py:66
  249.2 23.1 %copy-start.1 = (f32[512,512,1]{1,0,2:T(8,128)S(1)}, f32[512,512,1]{1,0,2:T(8,128)}, u32[]{:S(2)}) copy-start(f32[512,512,1]{1,0,2:T(8,128)} %constant.62) | copy-start | bytes 3145732
  275.9 58.7 %collective-permute-start.2 = (bf16[128,7168]{0,1:T(8,128)(2,1)S(1)}, bf16[128,7168]{0,1:T(8,128)(2,1)S(1)}, u32[]{:S(2)}, u32[]{:S(2)}) collective-permute-start(bf16[128,7168]{0,1:T(8,128)(2,1)S(1)} %bitcast_convert_fusion), channel_id=1, source_target_pairs={{0,1},{1,0},{2,3},{3,2},{4,5},{5,4},{6,7},{7,6},{8,9},{9,8},{10,11... | collective-permute-start | bytes 5505032 | tf_op jit(solution)/shard_map/ppermute | solution.py:10
  335.1 81.3 %collective-permute-start.3 = (bf16[128,7168]{0,1:T(8,128)(2,1)S(1)}, bf16[128,7168]{0,1:T(8,128)(2,1)S(1)}, u32[]{:S(2)}, u32[]{:S(2)}) collective-permute-start(bf16[128,7168]{0,1:T(8,128)(2,1)S(1)} %fusion.8), channel_id=1, source_target_pairs={{0,2},{1,3},{2,0},{3,1},{4,6},{5,7},{6,4},{7,5},{8,10},{9,11},{10,... | collective-permute-start | bytes 5505032 | tf_op jit(solution)/shard_map/ppermute | solution.py:10
Sparse Core Ops, SparseCore 0:
  65.0 66.0 all-gather.4
  165.8 51.7 all-gather.2
  219.9 49.0 reduce-scatter.4
  271.8 43.0 reduce-scatter.2
  317.9 490.1 all-reduce.1
where the time goes:
time: 835 us
  waiting for transfers between devices  715 us (86%)
  matrix products  52.1 us (6%)
  local copies, waits for them, and re-layouts  31.4 us (4%)
  between operations  13.9 us (2%)
  other arithmetic  12.2 us (1%)
  starting transfers between devices  10.2 us (1%)
    psum x1, waiting for transfers between devices, body(): lax.psum((grad_term * (1.0 / float(token_total) ** 0.5)).astype(jnp.bfloa...  388 us
    ppermute x4, waiting for transfers between devices, partner_2(): lax.ppermute(shard, axis, [(i, i ^ 1 << distance) for i in range(lax.axis...  272 us
    all_gather x1, waiting for transfers between devices, body(): gathered = lax.all_gather(rotated, 'seq', axis=0, tiled=True)  35.5 us
    unnamed x11, local copies, waits for them, and re-layouts  28.1 us
    reduce_scatter x1, waiting for transfers between devices, body(): lax.psum_scatter(lax.dot_general(grads_all, weight, (((1,), (1,)), ((), (...  19.8 us
  transfers between devices with their start and end apart: 9, of which 7 were waited for; matrix products, arithmetic and copies ran while one was open for 8% of the time, Pallas kernels for 0%

commit v1 on v0

v1 whole, which is shorter than its diff:
```python
import functools

import jax
import jax.numpy as jnp
from jax import lax
from jax.experimental import pallas as pl
from jax.experimental.pallas import tpu as pltpu
from jax.sharding import PartitionSpec as P

HB = 512
BF = jnp.bfloat16
F32 = jnp.float32
VMEM_BYTES = 40 * 1024 * 1024
HIDDEN_SPLIT = (4,4,3,3)
GRAD_SPLIT = (4,4,3,3)
def partner(shard, axis, bit):
    return lax.ppermute(shard, axis, [(i, i ^ 1 << bit) for i in range(lax.axis_size(axis))])


def bits_of(axis):
    return lax.axis_size(axis).bit_length() - 1


def walsh_table(table_order):
    matrix = jnp.ones((1, 1), F32)
    while matrix.shape[0] < table_order:
        matrix = jnp.concatenate(
            [jnp.concatenate([matrix, matrix], 1), jnp.concatenate([matrix, -matrix], 1)], 0
        )
    return matrix.astype(BF)


def split_blocks(total, sizes):
    if sum(sizes) != total:
        count = min(len(sizes), total)
        sizes = [total // count + (1 if i < total % count else 0) for i in range(count)]
    return [(sum(sizes[:i]), sizes[i]) for i in range(len(sizes))]


def call(kernel, grid, in_specs, out_specs, out_shape, flops, nbytes, scratch=(), aliases=None):
    return pl.pallas_call(
        kernel,
        grid=grid,
        in_specs=in_specs,
        out_specs=out_specs,
        out_shape=out_shape,
        scratch_shapes=list(scratch),
        input_output_aliases=aliases or {},
        compiler_params=pltpu.CompilerParams(vmem_limit_bytes=VMEM_BYTES),
        cost_estimate=pl.CostEstimate(flops=flops, bytes_accessed=nbytes, transcendentals=0),
    )


def sign_of(axis, bit):
    upper = lax.rem(lax.div(lax.axis_index(axis), 1 << bit), 2)
    return (1 - 2 * upper).astype(F32).reshape(1, 1)


SIGN_SPEC = pl.BlockSpec(memory_space=pltpu.SMEM)


def combine(sign, own, own_block, received):
    rows, width = received.shape
    blocks = width // HB

    def kernel(sign_ref, own_ref, received_ref, out_ref):
        out_ref[...] = (
            received_ref[...].astype(F32) + sign_ref[0, 0] * own_ref[...].astype(F32)
        ).astype(BF)

    return call(
        kernel,
        (blocks,),
        [
            SIGN_SPEC,
            pl.BlockSpec((rows, HB), lambda i: (0, own_block + i)),
            pl.BlockSpec((rows, HB), lambda i: (0, i)),
        ],
        pl.BlockSpec((rows, HB), lambda i: (0, i)),
        jax.ShapeDtypeStruct((rows, width), BF),
        2 * rows * width,
        6 * rows * width,
    )(sign, own, received)


def finish_hidden(sign, own, received, table, scale):
    rows, width = received.shape
    blocks = width // HB

    def kernel(sign_ref, own_ref, received_ref, table_ref, out_ref):
        mixed = received_ref[...].astype(F32) + sign_ref[0, 0] * own_ref[...].astype(F32)
        turned = lax.dot_general(
            table_ref[...], mixed.astype(BF), (((1,), (1,)), ((), ())), preferred_element_type=F32
        )
        out_ref[...] = (turned * scale).astype(BF)

    return call(
        kernel,
        (blocks,),
        [
            SIGN_SPEC,
            pl.BlockSpec((rows, HB), lambda i: (0, i)),
            pl.BlockSpec((rows, HB), lambda i: (0, i)),
            pl.BlockSpec((HB, HB), lambda i: (0, 0)),
        ],
        pl.BlockSpec((HB, rows), lambda i: (i, 0)),
        jax.ShapeDtypeStruct((width, rows), BF),
        2 * rows * width * HB,
        6 * rows * width,
    )(sign, own, received, table)


def finish_grad(sign, own, received, table, scale, first, total, result):
    rows, width = received.shape
    blocks = width // HB

    def kernel(sign_ref, own_ref, received_ref, table_ref, *refs):
        out_ref = refs[-1]
        mixed = received_ref[...].astype(F32) + sign_ref[0, 0] * own_ref[...].astype(F32)
        turned = jnp.dot(mixed.astype(BF), table_ref[...], preferred_element_type=F32)
        out_ref[...] = (turned * scale).astype(BF)

    args = [sign, own, received, table]
    specs = [
        SIGN_SPEC,
        pl.BlockSpec((rows, HB), lambda i: (0, i)),
        pl.BlockSpec((rows, HB), lambda i: (0, i)),
        pl.BlockSpec((HB, HB), lambda i: (0, 0)),
    ]
    aliases = None
    if result is not None:
        args.append(result)
        specs.append(pl.BlockSpec(memory_space=pl.ANY))
        aliases = {4: 0}
    return call(
        kernel,
        (blocks,),
        specs,
        pl.BlockSpec((rows, HB), lambda i: (0, first + i)),
        jax.ShapeDtypeStruct((rows, total), BF),
        2 * rows * width * HB,
        6 * rows * width,
        aliases=aliases,
    )(*args)


def rotated_grad_parts(grads, weight, first, blocks, count):
    tokens, columns = grads.shape
    rows = tokens // count

    def kernel(grads_ref, weight_ref, *out_refs):
        total = lax.dot_general(
            grads_ref[...], weight_ref[...], (((1,), (1,)), ((), ())), preferred_element_type=F32
        ).astype(BF)
        for n, out_ref in enumerate(out_refs):
            out_ref[...] = total[n * rows : (n + 1) * rows]

    return call(
        kernel,
        (blocks,),
        [
            pl.BlockSpec((tokens, columns), lambda i: (0, 0)),
            pl.BlockSpec((HB, columns), lambda i: (first + i, 0)),
        ],
        [pl.BlockSpec((rows, HB), lambda i: (0, i))] * count,
        [jax.ShapeDtypeStruct((rows, blocks * HB), BF)] * count,
        2 * tokens * columns * blocks * HB,
        2 * blocks * HB * columns,
    )(grads, weight)


def output_part(turned, weight, first, running, last):
    width, tokens = turned.shape
    columns = weight.shape[1]
    blocks = width // HB

    def kernel(turned_ref, weight_ref, *refs):
        total_ref = refs[-1]
        out_ref = refs[-2]
        step = pl.program_id(0)

        @pl.when(step == 0)
        def _():
            if running is None:
                total_ref[...] = jnp.zeros_like(total_ref)
            else:
                total_ref[...] = refs[0][...]

        total_ref[...] += lax.dot_general(
            turned_ref[...], weight_ref[...], (((0,), (0,)), ((), ())), preferred_element_type=F32
        )

        @pl.when(step == blocks - 1)
        def _():
            out_ref[...] = total_ref[...].astype(out_ref.dtype)

    whole = pl.BlockSpec((tokens, columns), lambda i: (0, 0))
    args = [turned, weight]
    specs = [
        pl.BlockSpec((HB, tokens), lambda i: (i, 0)),
        pl.BlockSpec((HB, columns), lambda i: (first + i, 0)),
    ]
    if running is not None:
        args.append(running)
        specs.append(whole)
    return call(
        kernel,
        (blocks,),
        specs,
        whole,
        jax.ShapeDtypeStruct((tokens, columns), BF if last else F32),
        2 * tokens * width * columns,
        2 * width * columns,
        scratch=[pltpu.VMEM((tokens, columns), F32)],
    )(*args)


def weight_grad_part(turned, grads, scale, first, total, result):
    width = turned[0].shape[0]
    columns = grads[0].shape[1]
    blocks = width // HB
    count = len(turned)
    tokens = sum(piece.shape[1] for piece in turned)

    def kernel(*refs):
        out_ref = refs[-1]
        left = jnp.concatenate([ref[...] for ref in refs[:count]], axis=1)
        right = jnp.concatenate([ref[...] for ref in refs[count : 2 * count]], axis=0)
        product = jnp.dot(left, right, preferred_element_type=F32)
        out_ref[...] = (product * scale).astype(BF)

    args = list(turned) + list(grads)
    specs = [pl.BlockSpec((HB, piece.shape[1]), lambda i: (i, 0)) for piece in turned]
    specs += [pl.BlockSpec(piece.shape, lambda i: (0, 0)) for piece in grads]
    aliases = None
    if result is not None:
        args.append(result)
        specs.append(pl.BlockSpec(memory_space=pl.ANY))
        aliases = {2 * count: 0}
    return call(
        kernel,
        (blocks,),
        specs,
        pl.BlockSpec((HB, columns), lambda i: (first + i, 0)),
        jax.ShapeDtypeStruct((total, columns), BF),
        2 * tokens * width * columns,
        2 * width * (columns + tokens),
        aliases=aliases,
    )(*args)


ORDER = [
    "G", "h1", "G", "h1", "h2", "G", "h0", "g1", "g0", "h2", "h1", "G",
    "g1", "g3", "h3", "h0", "h1", "h2", "h1", "g3", "h3", "g2", "g0", "h0",
    "h1", "g1", "g2", "G", "h3", "h1", "h2", "g3", "h2", "g1", "h0", "h3",
    "h0", "g2", "h3", "h2", "g3", "g0", "out", "h0", "g2", "h2", "h3", "h0",
    "out", "g0", "h3", "out",
]


def body(hidden, weight, out_grad):
    n_tensor, n_seq, n_dp = (lax.axis_size(a) for a in ("tensor", "seq", "dp"))
    me_tensor, me_seq = lax.axis_index("tensor"), lax.axis_index("seq")
    rows, features = hidden.shape
    blocks = features // HB
    per_seq = n_tensor // n_seq
    table = walsh_table(HB)
    norm_scale = 1.0 / float(n_tensor * HB) ** 0.5
    grad_scale = 1.0 / float(rows * n_seq * n_dp) ** 0.5
    signs = [sign_of("tensor", bit) for bit in range(bits_of("tensor"))]
    plus = jnp.ones((1, 1), F32)
    near_first = list(range(bits_of("tensor")))
    far_first = near_first[::-1]
    seq_bits = list(range(bits_of("seq")))
    dp_bits = list(reversed(range(bits_of("dp"))))
    hidden_parts = split_blocks(blocks, HIDDEN_SPLIT)
    grad_parts = split_blocks(blocks, GRAD_SPLIT)
    state = {"last": None, "running": None, "grad_weight": None, "grad_hidden": None}
    state["to_sum"] = len(hidden_parts)

    def tied(value):
        if state["last"] is None:
            return value
        return lax.optimization_barrier((value, state["last"]))[0]

    def done(value):
        state["last"] = value
        return value

    def send(value, axis, bit):
        return partner(tied(value), axis, bit)

    def gather_grads():
        grads = out_grad
        for bit in far_first:
            arrived = partner(grads, "tensor", bit)
            yield
            grads = done(jnp.concatenate([grads, arrived], axis=0))
        shards = grads.reshape(n_tensor, *out_grad.shape)

        def shard_of(owner):
            apart = owner ^ me_tensor
            place = sum(((apart >> b) & 1) << (len(near_first) - 1 - b) for b in near_first)
            return lax.dynamic_index_in_dim(shards, place, 0, keepdims=False)

        grads = done(
            jnp.concatenate(
                [
                    shard_of((me_seq ^ run) * per_seq + inner)
                    for run in range(n_seq)
                    for inner in range(per_seq)
                ],
                axis=0,
            )
        )
        state["grads"] = grads
        pieces = [grads]
        for bit in dp_bits:
            pieces += [send(piece, "dp", bit) for piece in pieces[::-1]][::-1]
            yield
            for piece in pieces[len(pieces) // 2 :]:
                done(piece)
        state["grad_pieces"] = pieces

    def hidden_part(first, size):
        own, own_block = hidden, first
        sent = tied(hidden)[:, first * HB : (first + size) * HB]
        for bit in far_first[:-1]:
            arrived = send(sent, "tensor", bit)
            yield
            own = done(combine(signs[bit], tied(own), own_block, arrived))
            sent, own_block = own, 0
        arrived = send(sent, "tensor", far_first[-1])
        yield
        turned = done(finish_hidden(signs[far_first[-1]], tied(sent), arrived, table, norm_scale))
        for bit in seq_bits:
            arrived = send(turned, "seq", bit)
            yield
            turned = done(jnp.concatenate([tied(turned), arrived], axis=1))
        pieces = [turned]
        for place, bit in enumerate(dp_bits):
            pieces += [send(piece, "dp", bit) for piece in pieces]
            yield
            if place == 0:
                state["to_sum"] -= 1
                state["running"] = done(
                    output_part(
                        tied(turned), weight, first, state["running"], state["to_sum"] == 0
                    )
                )
                yield
        state["grad_weight"] = done(
            weight_grad_part(
                [tied(pieces[0])] + pieces[1:],
                state["grad_pieces"],
                grad_scale,
                first,
                features,
                state["grad_weight"],
            )
        )

    def grad_part(first, size):
        terms = list(rotated_grad_parts(tied(state["grads"]), weight, first, size, n_seq))
        done(terms[0])
        for bit in reversed(seq_bits):
            half = len(terms) // 2
            arrived = [send(term, "seq", bit) for term in terms[half:]]
            yield
            terms = [
                done(combine(plus, tied(terms[n]), 0, arrived[n])) for n in range(half)
            ]
        own = terms[0]
        for bit in near_first[:-1]:
            arrived = send(own, "tensor", bit)
            yield
            own = done(combine(signs[bit], tied(own), 0, arrived))
        arrived = send(own, "tensor", near_first[-1])
        yield
        state["grad_hidden"] = done(
            finish_grad(
                signs[near_first[-1]],
                tied(own),
                arrived,
                table,
                norm_scale,
                first,
                features,
                state["grad_hidden"],
            )
        )

    def sum_output():
        shard_rows = out_grad.shape[0]
        runs = state["running"].reshape(n_tensor, shard_rows, -1)

        def run_for(apart):
            owner = me_tensor ^ apart
            place = ((owner // per_seq) ^ me_seq) * per_seq + owner % per_seq
            return lax.dynamic_index_in_dim(runs, place, 0, keepdims=False)

        sums = {apart: run_for(apart) for apart in range(n_tensor)}
        for bit in near_first:
            leaving = [apart for apart in sums if apart >> bit & 1]
            arrived = partner(jnp.concatenate([sums[a] for a in leaving], axis=0), "tensor", bit)
            yield
            arrived = tied(arrived)
            for place, apart in enumerate(leaving):
                block = arrived[place * shard_rows : (place + 1) * shard_rows]
                kept = apart ^ 1 << bit
                sums[kept] = (sums[kept].astype(F32) + block.astype(F32)).astype(BF)
                del sums[apart]
            done(sums[0])
        state["output"] = sums[0]

    steps = {"G": gather_grads()}
    for n, (first, size) in enumerate(hidden_parts):
        steps["h%d" % n] = hidden_part(first, size)
    for n, (first, size) in enumerate(grad_parts):
        steps["g%d" % n] = grad_part(first, size)
    steps["out"] = sum_output()
    order = ORDER
    if (n_tensor, n_seq, n_dp) != (4, 2, 4):
        order = ["G"] * 20
        for name in [n for n in steps if n[0] in "hg"]:
            order += [name] * 20
        order += ["out"] * 10
    for name in order:
        next(steps[name], None)
    return (state["output"], state["grad_hidden"], state["grad_weight"])


def solution(mesh):
    in_specs = (P(("dp", "seq"), "tensor"), P("tensor", "seq"), P(("dp", "tensor"), "seq"))
    out_specs = (P(("dp", "tensor"), "seq"), P(("dp", "seq"), "tensor"), P("tensor", "seq"))
    return jax.shard_map(body, mesh=mesh, in_specs=in_specs, out_specs=out_specs, check_vma=False)
```

time: 835 us -> 284 us (0.34)
  waiting for transfers between devices: 715 us -> 105 us
  Pallas kernels: 0 us -> 117 us
  matrix products: 52.1 us -> 0 us
  starting transfers between devices: 10.2 us -> 46.2 us
  local copies, waits for them, and re-layouts: 31.4 us -> 12 us
  between operations: 13.9 us -> 1.11 us
  other arithmetic: 12.2 us -> 1.11 us
    psum x1 -> x0, waiting for transfers between devices: 388 us -> none  [body(): lax.psum((grad_term * (1.0 / float(token_total) ** 0.5)).astype(jnp.bfloa...]
    ppermute x4 -> x43, waiting for transfers between devices: 272 us -> 105 us  [partner(): lax.ppermute(shard, axis, [(i, i ^ 1 << bit) for i in range(lax.axis_size...]
    pallas_call x0 -> x32, Pallas kernels: none -> 117 us  [the longest x4 43.8 us: weight_grad_part(): call(kernel, (blocks,), specs, pl.BlockSpec((HB, columns), lambda i: (fir...]
    dot_general x5 -> x0, matrix products: 52.1 us -> none  [the longest x1 16.6 us: body(): partial_sums = jnp.dot(gathered, weight, preferred_element_type=jnp.float32)]
    ppermute x4 -> x43, starting transfers between devices: 9.81 us -> 46.2 us  [partner(): lax.ppermute(shard, axis, [(i, i ^ 1 << bit) for i in range(lax.axis_size...]
    all_gather x2 -> x0, waiting for transfers between devices: 35.5 us -> none  [the longest x1 35.5 us: body(): gathered = lax.all_gather(rotated, 'seq', axis=0, tiled=True)]
    unnamed x11 -> x35, local copies, waits for them, and re-layouts: 28.1 us -> 6.46 us
    reduce_scatter x2 -> x0, waiting for transfers between devices: 19.8 us -> none  [the longest x1 19.8 us: body(): lax.psum_scatter(lax.dot_general(grads_all, weight, (((1,), (1,)), ((), (...]
  transfers between devices with their start and end apart: 9 -> 43, of which waited for: 7 -> 17; matrix products, arithmetic and copies ran while one was open for 8% -> 3% of each run, Pallas kernels for 0% -> 41%
where the time goes in v1:
time: 284 us; the launch traced here: 283 us
  Pallas kernels  117 us (41%)
  waiting for transfers between devices  105 us (37%)
  starting transfers between devices  46.2 us (16%)
  local copies, waits for them, and re-layouts  12 us (4%)
    ppermute x43, waiting for transfers between devices, partner(): lax.ppermute(shard, axis, [(i, i ^ 1 << bit) for i in range(lax.axis_size...  105 us
    ppermute x43, starting transfers between devices, partner(): lax.ppermute(shard, axis, [(i, i ^ 1 << bit) for i in range(lax.axis_size...  46.2 us
    pallas_call x4, Pallas kernels, weight_grad_part(): call(kernel, (blocks,), specs, pl.BlockSpec((HB, columns), lambda i: (fir...  43.8 us
    pallas_call x4, Pallas kernels, output_part(): call(kernel, (blocks,), specs, whole, jax.ShapeDtypeStruct((tokens, colum...  22.1 us
    pallas_call x4, Pallas kernels, rotated_grad_parts(): call(kernel, (blocks,), [pl.BlockSpec((tokens, columns), lambda i: (0, 0)...  21.4 us
    pallas_call x12, Pallas kernels, combine(): call(kernel, (blocks,), [SIGN_SPEC, pl.BlockSpec((rows, HB), lambda i: (0...  14.3 us
    pallas_call x4, Pallas kernels, finish_grad(): call(kernel, (blocks,), specs, pl.BlockSpec((rows, HB), lambda i: (0, fir...  9.36 us
    unnamed x35, local copies, waits for them, and re-layouts  6.46 us
  transfers between devices with their start and end apart: 43, of which 17 were waited for; matrix products, arithmetic and copies ran while one was open for 3% of the time, Pallas kernels for 41%

profile of v1, /device:TPU:0, one launch (start us, length us, event | category | flops | bytes accessed | tf_op | source)
XLA Modules:
  0.0 283.1 jit_solution(17779278440601798117)
XLA Ops:
  0.6 4.1 %collective-permute-start = (bf16[64,2048]{1,0:T(8,128)(2,1)}, bf16[64,2048]{1,0:T(8,128)(2,1)S(1)}, u32[]{:S(2)}, u32[]{:S(2)}) collective-permute-start(bf16[64,2048]{1,0:T(8,128)(2,1)} %param.5), channel_id=1, source_target_pairs={{0,2},{1,3},{2,0},{3,1},{4,6},{5,7},{6,4},{7,5},{8,10},{9,11},{10,... | collective-permute-start | bytes 786440 | tf_op jit(solution)/shard_map/ppermute | solution.py:17
  5.7 11.1 %collective-permute-done = bf16[64,2048]{1,0:T(8,128)(2,1)S(1)} collective-permute-done((bf16[64,2048]{1,0:T(8,128)(2,1)}, bf16[64,2048]{1,0:T(8,128)(2,1)S(1)}, u32[]{:S(2)}, u32[]{:S(2)}) %collective-permute-start) | collective-permute-done | bytes 262176 | tf_op jit(solution)/shard_map/ppermute | solution.py:17
  19.7 3.3 %collective-permute-start.4 = (bf16[128,2048]{1,0:T(8,128)(2,1)}, bf16[128,2048]{1,0:T(8,128)(2,1)S(1)}, u32[]{:S(2)}, u32[]{:S(2)}) collective-permute-start(bf16[128,2048]{1,0:T(8,128)(2,1)} %slice.18), channel_id=1, source_target_pairs={{0,2},{1,3},{2,0},{3,1},{4,6},{5,7},{6,4},{7,5},{8,10},{9,11},{10,... | collective-permute-start | bytes 1572872 | tf_op jit(solution)/shard_map/ppermute | solution.py:17
  22.9 16.0 %collective-permute-done.1 = bf16[128,2048]{1,0:T(8,128)(2,1)S(1)} collective-permute-done((bf16[128,2048]{1,0:T(8,128)(2,1)S(1)}, bf16[128,2048]{1,0:T(8,128)(2,1)S(1)}, u32[]{:S(2)}, u32[]{:S(2)}) %collective-permute-start.1) | collective-permute-done | bytes 524320 | tf_op jit(solution)/shard_map/ppermute | solution.py:17
  40.7 5.6 %collective-permute-done.4.received_ref = bf16[128,2048]{1,0:T(8,128)(2,1)S(1)} collective-permute-done((bf16[128,2048]{1,0:T(8,128)(2,1)}, bf16[128,2048]{1,0:T(8,128)(2,1)S(1)}, u32[]{:S(2)}, u32[]{:S(2)}) %collective-permute-start.4) | collective-permute-done | bytes 524320 | tf_op jit(solution)/shard_map/ppermute | solution.py:17
  48.6 2.9 %collective-permute-start.6 = (bf16[128,2048]{1,0:T(8,128)(2,1)}, bf16[128,2048]{1,0:T(8,128)(2,1)}, u32[]{:S(2)}, u32[]{:S(2)}) collective-permute-start(bf16[128,2048]{1,0:T(8,128)(2,1)} %shard_map.61.own_ref), channel_id=1, source_target_pairs={{0,1},{1,0},{2,3},{3,2},{4,5},{5,4},{6,7},{7,6},{8,9},{9,8},{10,11... | collective-permute-start | bytes 1572872 | tf_op jit(solution)/shard_map/ppermute | solution.py:17
  51.5 6.3 %shard_map.58 = (bf16[128,2048]{1,0:T(8,128)(2,1)S(1)}, bf16[128,2048]{1,0:T(8,128)(2,1)}) custom-call(bf16[256,2048]{1,0:T(8,128)(2,1)S(1)} %pad_maximum_fusion.1.grads_ref.refs_4_, bf16[7168,2048]{1,0:T(8,128)(2,1)} %weight_ref.15), custom_call_target="tpu_custom_call" | custom-call | flops 2147483648 | bytes 8388608 | tf_op jit(solution)/shard_map/pallas_call | solution.py:158
  61.0 5.6 %shard_map.62 = (bf16[128,2048]{1,0:T(8,128)(2,1)S(1)}, bf16[128,2048]{1,0:T(8,128)(2,1)S(1)}) custom-call(bf16[256,2048]{1,0:T(8,128)(2,1)S(1)} %pad_maximum_fusion.1.grads_ref.refs_4_, bf16[7168,2048]{1,0:T(8,128)(2,1)} %weight_ref.15), custom_call_target="tpu_custom_call" | custom-call | flops 2147483648 | bytes 8388608 | tf_op jit(solution)/shard_map/pallas_call | solution.py:158
  70.3 3.8 %collective-permute-done.6.received_ref = bf16[128,2048]{1,0:T(8,128)(2,1)} collective-permute-done((bf16[128,2048]{1,0:T(8,128)(2,1)}, bf16[128,2048]{1,0:T(8,128)(2,1)}, u32[]{:S(2)}, u32[]{:S(2)}) %collective-permute-start.6) | collective-permute-done | bytes 524320 | tf_op jit(solution)/shard_map/ppermute | solution.py:17
  74.2 2.9 %shard_map.64 = bf16[2048,128]{1,0:T(8,128)(2,1)S(1)} custom-call(f32[1,1]{1,0:T(1,128)} %bitcast.sign_ref, bf16[128,2048]{1,0:T(8,128)(2,1)} %shard_map.61.own_ref, bf16[128,2048]{1,0:T(8,128)(2,1)} %collective-permute-done.6.received_ref, bf16[512,512]{1,0:T(8,128)(2,1)S(1)} %copy-done.1), custom_call_target="tpu_custom_call" | custom-call | flops 268435456 | bytes 1572864 | tf_op jit(solution)/shard_map/pallas_call | solution.py:97
  80.8 4.7 %shard_map.60 = (bf16[128,1536]{1,0:T(8,128)(2,1)S(1)}, bf16[128,1536]{1,0:T(8,128)(2,1)S(1)}) custom-call(bf16[256,2048]{1,0:T(8,128)(2,1)S(1)} %pad_maximum_fusion.1.grads_ref.refs_4_, bf16[7168,2048]{1,0:T(8,128)(2,1)} %weight_ref.15), custom_call_target="tpu_custom_call" | custom-call | flops 1610612736 | bytes 6291456 | tf_op jit(solution)/shard_map/pallas_call | solution.py:158
  85.5 5.2 %collective-permute-done.7.received_ref = bf16[128,2048]{1,0:T(8,128)(2,1)} collective-permute-done((bf16[128,2048]{1,0:T(8,128)(2,1)}, bf16[128,2048]{1,0:T(8,128)(2,1)}, u32[]{:S(2)}, u32[]{:S(2)}) %collective-permute-start.7) | collective-permute-done | bytes 524320 | tf_op jit(solution)/shard_map/ppermute | solution.py:17
  98.6 12.6 %collective-permute-done.9.received_ref = bf16[128,1536]{1,0:T(8,128)(2,1)S(1)} collective-permute-done((bf16[128,1536]{1,0:T(8,128)(2,1)S(1)}, bf16[128,1536]{1,0:T(8,128)(2,1)S(1)}, u32[]{:S(2)}, u32[]{:S(2)}) %collective-permute-start.9) | collective-permute-done | bytes 393248 | tf_op jit(solution)/shard_map/ppermute | solution.py:17
  114.4 5.8 %shard_map.67.refs_0_ = f32[256,2048]{1,0:T(8,128)S(1)} custom-call(bf16[2048,256]{1,0:T(8,128)(2,1)S(1)} %constant_dynamic-update-slice_fusion.2.turned_ref.refs_0_, bf16[7168,2048]{1,0:T(8,128)(2,1)} %weight_ref.15), custom_call_target="tpu_custom_call" | custom-call | flops 2147483648 | bytes 8388608 | tf_op jit(solution)/shard_map/pallas_call | solution.py:206
  120.9 4.7 %shard_map.71 = (bf16[128,1536]{1,0:T(8,128)(2,1)S(1)}, bf16[128,1536]{1,0:T(8,128)(2,1)S(1)}) custom-call(bf16[256,2048]{1,0:T(8,128)(2,1)S(1)} %pad_maximum_fusion.1.grads_ref.refs_4_, bf16[7168,2048]{1,0:T(8,128)(2,1)} %weight_ref.15), custom_call_target="tpu_custom_call" | custom-call | flops 1610612736 | bytes 6291456 | tf_op jit(solution)/shard_map/pallas_call | solution.py:158
  129.7 7.9 %collective-permute-done.16.received_ref = bf16[128,2048]{1,0:T(8,128)(2,1)S(1)} collective-permute-done((bf16[128,2048]{1,0:T(8,128)(2,1)S(1)}, bf16[128,2048]{1,0:T(8,128)(2,1)S(1)}, u32[]{:S(2)}, u32[]{:S(2)}) %collective-permute-start.16) | collective-permute-done | bytes 524320 | tf_op jit(solution)/shard_map/ppermute | solution.py:17
  139.0 8.8 %collective-permute-done.26.received_ref = bf16[128,1536]{1,0:T(8,128)(2,1)S(1)} collective-permute-done((bf16[128,1536]{1,0:T(8,128)(2,1)S(1)}, bf16[128,1536]{1,0:T(8,128)(2,1)S(1)}, u32[]{:S(2)}, u32[]{:S(2)}) %collective-permute-start.26) | collective-permute-done | bytes 393248 | tf_op jit(solution)/shard_map/ppermute | solution.py:17
  149.9 7.1 %collective-permute-done.13.received_ref = bf16[128,1536]{1,0:T(8,128)(2,1)S(1)} collective-permute-done((bf16[128,1536]{1,0:T(8,128)(2,1)S(1)}, bf16[128,1536]{1,0:T(8,128)(2,1)S(1)}, u32[]{:S(2)}, u32[]{:S(2)}) %collective-permute-start.13) | collective-permute-done | bytes 393248 | tf_op jit(solution)/shard_map/ppermute | solution.py:17
  161.8 11.9 %shard_map.75.refs_8_ = bf16[7168,2048]{1,0:T(8,128)(2,1)} custom-call(bf16[2048,256]{1,0:T(8,128)(2,1)S(1)} %constant_dynamic-update-slice_fusion.2.turned_ref.refs_0_, bf16[2048,256]{1,0:T(8,128)(2,1)S(1)} %collective-permute-done.17.refs_1_, bf16[2048,256]{1,0:T(8,128)(2,1)S(1)} %collective-permute-done.18.refs_2_, ...), custom_call_target="tpu_custom_call" | custom-call | flops 8589934592 | bytes 12582912 | tf_op jit(solution)/shard_map/pallas_call | solution.py:240
  175.0 5.1 %collective-permute-done.22.received_ref = bf16[128,1536]{1,0:T(8,128)(2,1)S(1)} collective-permute-done((bf16[128,1536]{1,0:T(8,128)(2,1)S(1)}, bf16[128,1536]{1,0:T(8,128)(2,1)S(1)}, u32[]{:S(2)}, u32[]{:S(2)}) %collective-permute-start.22) | collective-permute-done | bytes 393248 | tf_op jit(solution)/shard_map/ppermute | solution.py:17
  182.1 5.1 %shard_map.77.refs_0_ = f32[256,2048]{1,0:T(8,128)S(1)} custom-call(bf16[1536,256]{1,0:T(8,128)(2,1)S(1)} %constant_dynamic-update-slice_fusion.4.turned_ref.refs_0_, bf16[7168,2048]{1,0:T(8,128)(2,1)} %weight_ref.15, f32[256,2048]{1,0:T(8,128)S(1)} %shard_map.67.refs_0_), custom_call_target="tpu_custom_call" | custom-call | flops 1610612736 | bytes 6291456 | tf_op jit(solution)/shard_map/pallas_call | solution.py:206
  196.7 3.4 %collective-permute-start.29 = (bf16[128,1536]{1,0:T(8,128)(2,1)S(1)}, bf16[128,1536]{1,0:T(8,128)(2,1)S(1)}, u32[]{:S(2)}, u32[]{:S(2)}) collective-permute-start(bf16[128,1536]{1,0:T(8,128)(2,1)S(1)} %shard_map.76.own_ref), channel_id=1, source_target_pairs={{0,2},{1,3},{2,0},{3,1},{4,6},{5,7},{6,4},{7,5},{8,10},{9,11},{10,... | collective-permute-start | bytes 1179656 | tf_op jit(solution)/shard_map/ppermute | solution.py:17
  200.1 6.0 %shard_map.80.refs_0_ = f32[256,2048]{1,0:T(8,128)S(1)} custom-call(bf16[2048,256]{1,0:T(8,128)(2,1)} %constant_dynamic-update-slice_fusion.6.turned_ref.refs_0_, bf16[7168,2048]{1,0:T(8,128)(2,1)} %weight_ref.15, f32[256,2048]{1,0:T(8,128)S(1)} %shard_map.77.refs_0_), custom_call_target="tpu_custom_call" | custom-call | flops 2147483648 | bytes 8388608 | tf_op jit(solution)/shard_map/pallas_call | solution.py:206
  207.6 5.1 %shard_map.82 = bf16[256,2048]{1,0:T(8,128)(2,1)S(1)} custom-call(bf16[1536,256]{1,0:T(8,128)(2,1)} %constant_dynamic-update-slice_fusion.8.turned_ref.refs_0_, bf16[7168,2048]{1,0:T(8,128)(2,1)} %weight_ref.15, f32[256,2048]{1,0:T(8,128)S(1)} %shard_map.80.refs_0_), custom_call_target="tpu_custom_call" | custom-call | flops 1610612736 | bytes 6291456 | tf_op jit(solution)/shard_map/pallas_call | solution.py:206
  214.4 3.4 %collective-permute-start.31 = (bf16[128,1536]{1,0:T(8,128)(2,1)}, bf16[128,1536]{1,0:T(8,128)(2,1)}, u32[]{:S(2)}, u32[]{:S(2)}) collective-permute-start(bf16[128,1536]{1,0:T(8,128)(2,1)} %shard_map.81.own_ref), channel_id=1, source_target_pairs={{0,2},{1,3},{2,0},{3,1},{4,6},{5,7},{6,4},{7,5},{8,10},{9,11},{10,... | collective-permute-start | bytes 1179656 | tf_op jit(solution)/shard_map/ppermute | solution.py:17
  224.2 4.1 %collective-permute-done.35.refs_1_ = bf16[2048,256]{1,0:T(8,128)(2,1)} collective-permute-done((bf16[2048,256]{1,0:T(8,128)(2,1)}, bf16[2048,256]{1,0:T(8,128)(2,1)}, u32[]{:S(2)}, u32[]{:S(2)}) %collective-permute-start.35) | collective-permute-done | bytes 1048608 | tf_op jit(solution)/shard_map/ppermute | solution.py:17
  228.3 8.1 %collective-permute-done.31.received_ref = bf16[128,1536]{1,0:T(8,128)(2,1)} collective-permute-done((bf16[128,1536]{1,0:T(8,128)(2,1)}, bf16[128,1536]{1,0:T(8,128)(2,1)}, u32[]{:S(2)}, u32[]{:S(2)}) %collective-permute-start.31) | collective-permute-done | bytes 393248 | tf_op jit(solution)/shard_map/ppermute | solution.py:17
  236.9 3.3 %shard_map.85.refs_0_ = bf16[128,7168]{1,0:T(8,128)(2,1)} custom-call(f32[1,1]{1,0:T(1,128)} %bitcast.1.sign_ref, bf16[128,1536]{1,0:T(8,128)(2,1)} %shard_map.81.own_ref, bf16[128,1536]{1,0:T(8,128)(2,1)} %collective-permute-done.31.received_ref, bf16[512,512]{1,0:T(8,128)(2,1)S(1)} %copy-done.1, ...), custom_call_target="tpu_custom_call", output_to_operand_aliasing={{}: (4, {})} | custom-call | flops 201326592 | bytes 1179648 | tf_op jit(solution)/shard_map/pallas_call | solution.py:135
  242.2 10.0 %shard_map.86.refs_8_ = bf16[7168,2048]{1,0:T(8,128)(2,1)} custom-call(bf16[1536,256]{1,0:T(8,128)(2,1)S(1)} %constant_dynamic-update-slice_fusion.4.turned_ref.refs_0_, bf16[1536,256]{1,0:T(8,128)(2,1)} %collective-permute-done.32.refs_1_, bf16[1536,256]{1,0:T(8,128)(2,1)} %collective-permute-done.33.refs_2_, ...), custom_call_target="tpu_custom_call", output_to_operand_aliasing={{}: (8, {})} | custom-call | flops 6442450944 | bytes 9437184 | tf_op jit(solution)/shard_map/pallas_call | solution.py:240
  252.2 3.8 %collective-permute-done.40.refs_1_ = bf16[1536,256]{1,0:T(8,128)(2,1)S(1)} collective-permute-done((bf16[1536,256]{1,0:T(8,128)(2,1)}, bf16[1536,256]{1,0:T(8,128)(2,1)S(1)}, u32[]{:S(2)}, u32[]{:S(2)}) %collective-permute-start.40) | collective-permute-done | bytes 786464 | tf_op jit(solution)/shard_map/ppermute | solution.py:17
  256.5 12.1 %shard_map.87.refs_8_ = bf16[7168,2048]{1,0:T(8,128)(2,1)} custom-call(bf16[2048,256]{1,0:T(8,128)(2,1)} %constant_dynamic-update-slice_fusion.6.turned_ref.refs_0_, bf16[2048,256]{1,0:T(8,128)(2,1)} %collective-permute-done.35.refs_1_, bf16[2048,256]{1,0:T(8,128)(2,1)S(1)} %collective-permute-done.36.refs_2_, ...), custom_call_target="tpu_custom_call", output_to_operand_aliasing={{}: (8, {})} | custom-call | flops 8589934592 | bytes 12582912 | tf_op jit(solution)/shard_map/pallas_call | solution.py:240
  271.0 9.7 %shard_map.89 = bf16[7168,2048]{1,0:T(8,128)(2,1)} custom-call(bf16[1536,256]{1,0:T(8,128)(2,1)} %constant_dynamic-update-slice_fusion.8.turned_ref.refs_0_, bf16[1536,256]{1,0:T(8,128)(2,1)S(1)} %collective-permute-done.40.refs_1_, bf16[1536,256]{1,0:T(8,128)(2,1)S(1)} %collective-permute-done.41.refs_2_, ...), custom_call_target="tpu_custom_call", output_to_operand_aliasing={{}: (8, {})} | custom-call | flops 6442450944 | bytes 9437184 | tf_op jit(solution)/shard_map/pallas_call | solution.py:240
  (137 shorter events, 72.2 us)
Async XLA Ops:
  16.9 22.1 %collective-permute-start.1 = (bf16[128,2048]{1,0:T(8,128)(2,1)S(1)}, bf16[128,2048]{1,0:T(8,128)(2,1)S(1)}, u32[]{:S(2)}, u32[]{:S(2)}) collective-permute-start(bf16[128,2048]{1,0:T(8,128)(2,1)S(1)} %constant_dynamic-update-slice_fusion), channel_id=1, source_target_pairs={{0,1},{1,0},{2,3},{3,2},{4,5},{5,4},{6,7},{7,6},{8,9},{9,8},{10,11... | collective-permute-start | bytes 1572872 | tf_op jit(solution)/shard_map/ppermute | solution.py:17
  19.7 26.6 %collective-permute-start.4 = (bf16[128,2048]{1,0:T(8,128)(2,1)}, bf16[128,2048]{1,0:T(8,128)(2,1)S(1)}, u32[]{:S(2)}, u32[]{:S(2)}) collective-permute-start(bf16[128,2048]{1,0:T(8,128)(2,1)} %slice.18), channel_id=1, source_target_pairs={{0,2},{1,3},{2,0},{3,1},{4,6},{5,7},{6,4},{7,5},{8,10},{9,11},{10,... | collective-permute-start | bytes 1572872 | tf_op jit(solution)/shard_map/ppermute | solution.py:17
  39.3 39.4 %collective-permute-start.2 = (bf16[256,2048]{1,0:T(8,128)(2,1)S(1)}, bf16[256,2048]{1,0:T(8,128)(2,1)}, u32[]{:S(2)}, u32[]{:S(2)}) collective-permute-start(bf16[256,2048]{1,0:T(8,128)(2,1)S(1)} %pad_maximum_fusion.1.grads_ref.refs_4_), channel_id=1, source_target_pairs={{0,16},{8,24},{16,0},{24,8},{1,17},{9,25},{17,1},{25,9},{2,18},{10... | collective-permute-start | bytes 3145736 | tf_op jit(solution)/shard_map/ppermute | solution.py:17
  48.6 19.8 %collective-permute-start.5 = (bf16[128,1536]{1,0:T(8,128)(2,1)}, bf16[128,1536]{1,0:T(8,128)(2,1)}, u32[]{:S(2)}, u32[]{:S(2)}) collective-permute-start(bf16[128,1536]{1,0:T(8,128)(2,1)} %slice.19), channel_id=1, source_target_pairs={{0,2},{1,3},{2,0},{3,1},{4,6},{5,7},{6,4},{7,5},{8,10},{9,11},{10,... | collective-permute-start | bytes 1179656 | tf_op jit(solution)/shard_map/ppermute | solution.py:17
  48.6 25.6 %collective-permute-start.6 = (bf16[128,2048]{1,0:T(8,128)(2,1)}, bf16[128,2048]{1,0:T(8,128)(2,1)}, u32[]{:S(2)}, u32[]{:S(2)}) collective-permute-start(bf16[128,2048]{1,0:T(8,128)(2,1)} %shard_map.61.own_ref), channel_id=1, source_target_pairs={{0,1},{1,0},{2,3},{3,2},{4,5},{5,4},{6,7},{7,6},{8,9},{9,8},{10,11... | collective-permute-start | bytes 1572872 | tf_op jit(solution)/shard_map/ppermute | solution.py:17
  58.7 20.0 %collective-permute-start.3 = (bf16[128,2048]{1,0:T(8,128)(2,1)}, bf16[128,2048]{1,0:T(8,128)(2,1)}, u32[]{:S(2)}, u32[]{:S(2)}) collective-permute-start(bf16[128,2048]{1,0:T(8,128)(2,1)} %get-tuple-element.92), channel_id=1, source_target_pairs={{0,4},{4,0},{1,5},{5,1},{2,6},{6,2},{3,7},{7,3},{8,12},{12,8},{9,1... | collective-permute-start | bytes 1572872 | tf_op jit(solution)/shard_map/ppermute | solution.py:17
  61.0 29.7 %collective-permute-start.7 = (bf16[128,2048]{1,0:T(8,128)(2,1)}, bf16[128,2048]{1,0:T(8,128)(2,1)}, u32[]{:S(2)}, u32[]{:S(2)}) collective-permute-start(bf16[128,2048]{1,0:T(8,128)(2,1)} %slice.20), channel_id=1, source_target_pairs={{0,2},{1,3},{2,0},{3,1},{4,6},{5,7},{6,4},{7,5},{8,10},{9,11},{10,... | collective-permute-start | bytes 1572872 | tf_op jit(solution)/shard_map/ppermute | solution.py:17
  93.0 36.3 %collective-permute-start.17 = (bf16[2048,256]{1,0:T(8,128)(2,1)S(1)}, bf16[2048,256]{1,0:T(8,128)(2,1)S(1)}, u32[]{:S(2)}, u32[]{:S(2)}) collective-permute-start(bf16[2048,256]{1,0:T(8,128)(2,1)S(1)} %constant_dynamic-update-slice_fusion.2.turned_ref.refs_0_), channel_id=1, source_target_pairs={{0,16},{8,24},{16,0},{24,8},{1,17},{9,25},{17,1},{25,9},{2,18},{10... | collective-permute-start | bytes 3145736 | tf_op jit(solution)/shard_map/ppermute | solution.py:17
  94.5 17.7 %collective-permute-start.10 = (bf16[128,1536]{1,0:T(8,128)(2,1)S(1)}, bf16[128,1536]{1,0:T(8,128)(2,1)S(1)}, u32[]{:S(2)}, u32[]{:S(2)}) collective-permute-start(bf16[128,1536]{1,0:T(8,128)(2,1)S(1)} %get-tuple-element.113), channel_id=1, source_target_pairs={{0,4},{4,0},{1,5},{5,1},{2,6},{6,2},{3,7},{7,3},{8,12},{12,8},{9,1... | collective-permute-start | bytes 1179656 | tf_op jit(solution)/shard_map/ppermute | solution.py:17
  96.1 24.4 %collective-permute-start.11 = (bf16[128,1536]{1,0:T(8,128)(2,1)S(1)}, bf16[128,1536]{1,0:T(8,128)(2,1)S(1)}, u32[]{:S(2)}, u32[]{:S(2)}) collective-permute-start(bf16[128,1536]{1,0:T(8,128)(2,1)S(1)} %slice.21), channel_id=1, source_target_pairs={{0,2},{1,3},{2,0},{3,1},{4,6},{5,7},{6,4},{7,5},{8,10},{9,11},{10,... | collective-permute-start | bytes 1179656 | tf_op jit(solution)/shard_map/ppermute | solution.py:17
  98.1 27.5 %collective-permute-start.14 = (bf16[128,2048]{1,0:T(8,128)(2,1)S(1)}, bf16[128,2048]{1,0:T(8,128)(2,1)S(1)}, u32[]{:S(2)}, u32[]{:S(2)}) collective-permute-start(bf16[128,2048]{1,0:T(8,128)(2,1)S(1)} %get-tuple-element.123), channel_id=1, source_target_pairs={{0,4},{4,0},{1,5},{5,1},{2,6},{6,2},{3,7},{7,3},{8,12},{12,8},{9,1... | collective-permute-start | bytes 1572872 | tf_op jit(solution)/shard_map/ppermute | solution.py:17
  112.3 25.3 %collective-permute-start.16 = (bf16[128,2048]{1,0:T(8,128)(2,1)S(1)}, bf16[128,2048]{1,0:T(8,128)(2,1)S(1)}, u32[]{:S(2)}, u32[]{:S(2)}) collective-permute-start(bf16[128,2048]{1,0:T(8,128)(2,1)S(1)} %shard_map.59.own_ref), channel_id=1, source_target_pairs={{0,1},{1,0},{2,3},{3,2},{4,5},{5,4},{6,7},{7,6},{8,9},{9,8},{10,11... | collective-permute-start | bytes 1572872 | tf_op jit(solution)/shard_map/ppermute | solution.py:17
  120.5 27.9 %collective-permute-start.12 = (bf16[256,2048]{1,0:T(8,128)(2,1)}, bf16[256,2048]{1,0:T(8,128)(2,1)S(1)}, u32[]{:S(2)}, u32[]{:S(2)}) collective-permute-start(bf16[256,2048]{1,0:T(8,128)(2,1)} %collective-permute-done.2.refs_5_), channel_id=1, source_target_pairs={{0,8},{8,0},{16,24},{24,16},{1,9},{9,1},{17,25},{25,17},{2,10},{10... | collective-permute-start | bytes 3145736 | tf_op jit(solution)/shard_map/ppermute | solution.py:17
  125.6 32.6 %collective-permute-start.20 = (bf16[256,2048]{1,0:T(8,128)(2,1)S(1)}, bf16[256,2048]{1,0:T(8,128)(2,1)S(1)}, u32[]{:S(2)}, u32[]{:S(2)}) collective-permute-start(bf16[256,2048]{1,0:T(8,128)(2,1)S(1)} %pad_maximum_fusion.1.grads_ref.refs_4_), channel_id=1, source_target_pairs={{0,8},{8,0},{16,24},{24,16},{1,9},{9,1},{17,25},{25,17},{2,10},{10... | collective-permute-start | bytes 3145736 | tf_op jit(solution)/shard_map/ppermute | solution.py:17
  129.1 31.0 %collective-permute-start.18 = (bf16[2048,256]{1,0:T(8,128)(2,1)S(1)}, bf16[2048,256]{1,0:T(8,128)(2,1)S(1)}, u32[]{:S(2)}, u32[]{:S(2)}) collective-permute-start(bf16[2048,256]{1,0:T(8,128)(2,1)S(1)} %constant_dynamic-update-slice_fusion.2.turned_ref.refs_0_), channel_id=1, source_target_pairs={{0,8},{8,0},{16,24},{24,16},{1,9},{9,1},{17,25},{25,17},{2,10},{10... | collective-permute-start | bytes 3145736 | tf_op jit(solution)/shard_map/ppermute | solution.py:17
  129.3 31.0 %collective-permute-start.19 = (bf16[2048,256]{1,0:T(8,128)(2,1)S(1)}, bf16[2048,256]{1,0:T(8,128)(2,1)S(1)}, u32[]{:S(2)}, u32[]{:S(2)}) collective-permute-start(bf16[2048,256]{1,0:T(8,128)(2,1)S(1)} %collective-permute-done.17.refs_1_), channel_id=1, source_target_pairs={{0,8},{8,0},{16,24},{24,16},{1,9},{9,1},{17,25},{25,17},{2,10},{10... | collective-permute-start | bytes 3145736 | tf_op jit(solution)/shard_map/ppermute | solution.py:17
  148.4 25.4 %collective-permute-start.21 = (bf16[1536,128]{1,0:T(8,128)(2,1)S(1)}, bf16[1536,128]{1,0:T(8,128)(2,1)S(1)}, u32[]{:S(2)}, u32[]{:S(2)}) collective-permute-start(bf16[1536,128]{1,0:T(8,128)(2,1)S(1)} %shard_map.66), channel_id=1, source_target_pairs={{0,4},{4,0},{1,5},{5,1},{2,6},{6,2},{3,7},{7,3},{8,12},{12,8},{9,1... | collective-permute-start | bytes 1179656 | tf_op jit(solution)/shard_map/ppermute | solution.py:17
  157.0 23.1 %collective-permute-start.22 = (bf16[128,1536]{1,0:T(8,128)(2,1)S(1)}, bf16[128,1536]{1,0:T(8,128)(2,1)S(1)}, u32[]{:S(2)}, u32[]{:S(2)}) collective-permute-start(bf16[128,1536]{1,0:T(8,128)(2,1)S(1)} %shard_map.68.own_ref), channel_id=1, source_target_pairs={{0,1},{1,0},{2,3},{3,2},{4,5},{5,4},{6,7},{7,6},{8,9},{9,8},{10,11... | collective-permute-start | bytes 1179656 | tf_op jit(solution)/shard_map/ppermute | solution.py:17
  158.3 63.4 %collective-permute-start.30 = (bf16[128,2048]{1,0:T(8,128)(2,1)}, bf16[128,2048]{1,0:T(8,128)(2,1)}, u32[]{:S(2)}, u32[]{:S(2)}) collective-permute-start(bf16[128,2048]{1,0:T(8,128)(2,1)} %shard_map.72.own_ref), channel_id=1, source_target_pairs={{0,1},{1,0},{2,3},{3,2},{4,5},{5,4},{6,7},{7,6},{8,9},{9,8},{10,11... | collective-permute-start | bytes 1572872 | tf_op jit(solution)/shard_map/ppermute | solution.py:17
  160.2 29.1 %collective-permute-start.23 = (bf16[128,2048]{1,0:T(8,128)(2,1)S(1)}, bf16[128,2048]{1,0:T(8,128)(2,1)S(1)}, u32[]{:S(2)}, u32[]{:S(2)}) collective-permute-start(bf16[128,2048]{1,0:T(8,128)(2,1)S(1)} %shard_map.74.own_ref), channel_id=1, source_target_pairs={{0,2},{1,3},{2,0},{3,1},{4,6},{5,7},{6,4},{7,5},{8,10},{9,11},{10,... | collective-permute-start | bytes 1572872 | tf_op jit(solution)/shard_map/ppermute | solution.py:17
  160.3 31.9 %collective-permute-start.24 = (bf16[2048,128]{1,0:T(8,128)(2,1)S(1)}, bf16[2048,128]{1,0:T(8,128)(2,1)S(1)}, u32[]{:S(2)}, u32[]{:S(2)}) collective-permute-start(bf16[2048,128]{1,0:T(8,128)(2,1)S(1)} %shard_map.73), channel_id=1, source_target_pairs={{0,4},{4,0},{1,5},{5,1},{2,6},{6,2},{3,7},{7,3},{8,12},{12,8},{9,1... | collective-permute-start | bytes 1572872 | tf_op jit(solution)/shard_map/ppermute | solution.py:17
  173.8 32.4 %collective-permute-start.27 = (bf16[128,1536]{1,0:T(8,128)(2,1)S(1)}, bf16[128,1536]{1,0:T(8,128)(2,1)S(1)}, u32[]{:S(2)}, u32[]{:S(2)}) collective-permute-start(bf16[128,1536]{1,0:T(8,128)(2,1)S(1)} %shard_map.79.own_ref), channel_id=1, source_target_pairs={{0,1},{1,0},{2,3},{3,2},{4,5},{5,4},{6,7},{7,6},{8,9},{9,8},{10,11... | collective-permute-start | bytes 1179656 | tf_op jit(solution)/shard_map/ppermute | solution.py:17
  193.1 20.6 %collective-permute-start.32 = (bf16[1536,256]{1,0:T(8,128)(2,1)S(1)}, bf16[1536,256]{1,0:T(8,128)(2,1)}, u32[]{:S(2)}, u32[]{:S(2)}) collective-permute-start(bf16[1536,256]{1,0:T(8,128)(2,1)S(1)} %constant_dynamic-update-slice_fusion.4.turned_ref.refs_0_), channel_id=1, source_target_pairs={{0,16},{8,24},{16,0},{24,8},{1,17},{9,25},{17,1},{25,9},{2,18},{10... | collective-permute-start | bytes 2359304 | tf_op jit(solution)/shard_map/ppermute | solution.py:17
  193.6 34.6 %collective-permute-start.35 = (bf16[2048,256]{1,0:T(8,128)(2,1)}, bf16[2048,256]{1,0:T(8,128)(2,1)}, u32[]{:S(2)}, u32[]{:S(2)}) collective-permute-start(bf16[2048,256]{1,0:T(8,128)(2,1)} %constant_dynamic-update-slice_fusion.6.turned_ref.refs_0_), channel_id=1, source_target_pairs={{0,16},{8,24},{16,0},{24,8},{1,17},{9,25},{17,1},{25,9},{2,18},{10... | collective-permute-start | bytes 3145736 | tf_op jit(solution)/shard_map/ppermute | solution.py:17
  212.8 27.5 %collective-permute-start.33 = (bf16[1536,256]{1,0:T(8,128)(2,1)S(1)}, bf16[1536,256]{1,0:T(8,128)(2,1)}, u32[]{:S(2)}, u32[]{:S(2)}) collective-permute-start(bf16[1536,256]{1,0:T(8,128)(2,1)S(1)} %constant_dynamic-update-slice_fusion.4.turned_ref.refs_0_), channel_id=1, source_target_pairs={{0,8},{8,0},{16,24},{24,16},{1,9},{9,1},{17,25},{25,17},{2,10},{10... | collective-permute-start | bytes 2359304 | tf_op jit(solution)/shard_map/ppermute | solution.py:17
  213.7 26.6 %collective-permute-start.34 = (bf16[1536,256]{1,0:T(8,128)(2,1)}, bf16[1536,256]{1,0:T(8,128)(2,1)}, u32[]{:S(2)}, u32[]{:S(2)}) collective-permute-start(bf16[1536,256]{1,0:T(8,128)(2,1)} %collective-permute-done.32.refs_1_), channel_id=1, source_target_pairs={{0,8},{8,0},{16,24},{24,16},{1,9},{9,1},{17,25},{25,17},{2,10},{10... | collective-permute-start | bytes 2359304 | tf_op jit(solution)/shard_map/ppermute | solution.py:17
  214.4 21.9 %collective-permute-start.31 = (bf16[128,1536]{1,0:T(8,128)(2,1)}, bf16[128,1536]{1,0:T(8,128)(2,1)}, u32[]{:S(2)}, u32[]{:S(2)}) collective-permute-start(bf16[128,1536]{1,0:T(8,128)(2,1)} %shard_map.81.own_ref), channel_id=1, source_target_pairs={{0,2},{1,3},{2,0},{3,1},{4,6},{5,7},{6,4},{7,5},{8,10},{9,11},{10,... | collective-permute-start | bytes 1179656 | tf_op jit(solution)/shard_map/ppermute | solution.py:17
  223.9 32.1 %collective-permute-start.36 = (bf16[2048,256]{1,0:T(8,128)(2,1)}, bf16[2048,256]{1,0:T(8,128)(2,1)S(1)}, u32[]{:S(2)}, u32[]{:S(2)}) collective-permute-start(bf16[2048,256]{1,0:T(8,128)(2,1)} %constant_dynamic-update-slice_fusion.6.turned_ref.refs_0_), channel_id=1, source_target_pairs={{0,8},{8,0},{16,24},{24,16},{1,9},{9,1},{17,25},{25,17},{2,10},{10... | collective-permute-start | bytes 3145736 | tf_op jit(solution)/shard_map/ppermute | solution.py:17
  228.2 28.2 %collective-permute-start.37 = (bf16[2048,256]{1,0:T(8,128)(2,1)}, bf16[2048,256]{1,0:T(8,128)(2,1)S(1)}, u32[]{:S(2)}, u32[]{:S(2)}) collective-permute-start(bf16[2048,256]{1,0:T(8,128)(2,1)} %collective-permute-done.35.refs_1_), channel_id=1, source_target_pairs={{0,8},{8,0},{16,24},{24,16},{1,9},{9,1},{17,25},{25,17},{2,10},{10... | collective-permute-start | bytes 3145736 | tf_op jit(solution)/shard_map/ppermute | solution.py:17
  236.3 19.6 %collective-permute-start.40 = (bf16[1536,256]{1,0:T(8,128)(2,1)}, bf16[1536,256]{1,0:T(8,128)(2,1)S(1)}, u32[]{:S(2)}, u32[]{:S(2)}) collective-permute-start(bf16[1536,256]{1,0:T(8,128)(2,1)} %constant_dynamic-update-slice_fusion.8.turned_ref.refs_0_), channel_id=1, source_target_pairs={{0,16},{8,24},{16,0},{24,8},{1,17},{9,25},{17,1},{25,9},{2,18},{10... | collective-permute-start | bytes 2359304 | tf_op jit(solution)/shard_map/ppermute | solution.py:17
  240.2 28.4 %collective-permute-start.28 = (bf16[128,2048]{1,0:T(8,128)(2,1)S(1)}, bf16[128,2048]{1,0:T(8,128)(2,1)S(1)}, u32[]{:S(2)}, u32[]{:S(2)}) collective-permute-start(bf16[128,2048]{1,0:T(8,128)(2,1)S(1)} %pad_maximum_fusion.2), channel_id=1, source_target_pairs={{0,1},{1,0},{2,3},{3,2},{4,5},{5,4},{6,7},{7,6},{8,9},{9,8},{10,11... | collective-permute-start | bytes 1572872 | tf_op jit(solution)/shard_map/ppermute | solution.py:17
  240.3 28.6 %collective-permute-start.39 = (bf16[128,2048]{1,0:T(8,128)(2,1)S(1)}, bf16[128,2048]{1,0:T(8,128)(2,1)S(1)}, u32[]{:S(2)}, u32[]{:S(2)}) collective-permute-start(bf16[128,2048]{1,0:T(8,128)(2,1)S(1)} %shard_map.84.own_ref), channel_id=1, source_target_pairs={{0,2},{1,3},{2,0},{3,1},{4,6},{5,7},{6,4},{7,5},{8,10},{9,11},{10,... | collective-permute-start | bytes 1572872 | tf_op jit(solution)/shard_map/ppermute | solution.py:17
  (26 other events, 327.4 us)

commit v2 on v1

--- a/solution.py
+++ b/solution.py
@@ -11,8 +11,9 @@
 BF = jnp.bfloat16
 F32 = jnp.float32
 VMEM_BYTES = 40 * 1024 * 1024
-HIDDEN_SPLIT = (4,4,3,3)
-GRAD_SPLIT = (4,4,3,3)
+HIDDEN_SPLIT = (3, 3, 4, 4)
+GRAD_SPLIT = (3, 3, 4, 4)
+PLANNED = {'weight_grad': 0.01, 'combine': 0.01}
 def partner(shard, axis, bit):
     return lax.ppermute(shard, axis, [(i, i ^ 1 << bit) for i in range(lax.axis_size(axis))])
 
@@ -37,9 +38,11 @@
     return [(sum(sizes[:i]), sizes[i]) for i in range(len(sizes))]
 
 
-def call(kernel, grid, in_specs, out_specs, out_shape, flops, nbytes, scratch=(), aliases=None):
+def call(name, kernel, grid, in_specs, out_specs, out_shape, flops, nbytes, scratch=(), aliases=None):
+    weight = PLANNED.get(name, 1)
     return pl.pallas_call(
         kernel,
+        name=name,
         grid=grid,
         in_specs=in_specs,
         out_specs=out_specs,
@@ -47,7 +50,7 @@
         scratch_shapes=list(scratch),
         input_output_aliases=aliases or {},
         compiler_params=pltpu.CompilerParams(vmem_limit_bytes=VMEM_BYTES),
-        cost_estimate=pl.CostEstimate(flops=flops, bytes_accessed=nbytes, transcendentals=0),
+        cost_estimate=pl.CostEstimate(flops=int(flops * weight), bytes_accessed=int(nbytes * weight), transcendentals=0),
     )
 
 
@@ -59,24 +62,29 @@
 SIGN_SPEC = pl.BlockSpec(memory_space=pltpu.SMEM)
 
 
-def combine(sign, own, own_block, received):
+def steps_for(first, blocks, least, unit):
+    for steps in range(least, blocks + 1):
+        size = blocks * HB // steps
+        if size * steps == blocks * HB and size % unit == 0 and first * HB % size == 0:
+            return steps, size, first * HB // size
+    return blocks, HB, first
+
+
+def combine(sign, own, received):
     rows, width = received.shape
-    blocks = width // HB
 
     def kernel(sign_ref, own_ref, received_ref, out_ref):
         out_ref[...] = (
             received_ref[...].astype(F32) + sign_ref[0, 0] * own_ref[...].astype(F32)
         ).astype(BF)
 
-    return call(
-        kernel,
-        (blocks,),
-        [
-            SIGN_SPEC,
-            pl.BlockSpec((rows, HB), lambda i: (0, own_block + i)),
-            pl.BlockSpec((rows, HB), lambda i: (0, i)),
-        ],
-        pl.BlockSpec((rows, HB), lambda i: (0, i)),
+    whole = pl.BlockSpec((rows, width), lambda i: (0, 0))
+    return call(
+        "combine",
+        kernel,
+        (1,),
+        [SIGN_SPEC, whole, whole],
+        whole,
         jax.ShapeDtypeStruct((rows, width), BF),
         2 * rows * width,
         6 * rows * width,
@@ -85,25 +93,26 @@
 
 def finish_hidden(sign, own, received, table, scale):
     rows, width = received.shape
-    blocks = width // HB
 
     def kernel(sign_ref, own_ref, received_ref, table_ref, out_ref):
-        mixed = received_ref[...].astype(F32) + sign_ref[0, 0] * own_ref[...].astype(F32)
-        turned = lax.dot_general(
-            table_ref[...], mixed.astype(BF), (((1,), (1,)), ((), ())), preferred_element_type=F32
-        )
-        out_ref[...] = (turned * scale).astype(BF)
-
-    return call(
-        kernel,
-        (blocks,),
-        [
-            SIGN_SPEC,
-            pl.BlockSpec((rows, HB), lambda i: (0, i)),
-            pl.BlockSpec((rows, HB), lambda i: (0, i)),
-            pl.BlockSpec((HB, HB), lambda i: (0, 0)),
-        ],
-        pl.BlockSpec((HB, rows), lambda i: (i, 0)),
+        for at in range(0, width, HB):
+            run = slice(at, at + HB)
+            mixed = received_ref[:, run].astype(F32) + sign_ref[0, 0] * own_ref[:, run].astype(F32)
+            turned = lax.dot_general(
+                table_ref[...],
+                mixed.astype(BF),
+                (((1,), (1,)), ((), ())),
+                preferred_element_type=F32,
+            )
+            out_ref[run, :] = (turned * scale).astype(BF)
+
+    whole = pl.BlockSpec((rows, width), lambda i: (0, 0))
+    return call(
+        "finish_hidden",
+        kernel,
+        (1,),
+        [SIGN_SPEC, whole, whole, pl.BlockSpec((HB, HB), lambda i: (0, 0))],
+        pl.BlockSpec((width, rows), lambda i: (0, 0)),
         jax.ShapeDtypeStruct((width, rows), BF),
         2 * rows * width * HB,
         6 * rows * width,
@@ -112,19 +121,21 @@
 
 def finish_grad(sign, own, received, table, scale, first, total, result):
     rows, width = received.shape
-    blocks = width // HB
+    steps, size, start = steps_for(first, width // HB, 1, HB)
 
     def kernel(sign_ref, own_ref, received_ref, table_ref, *refs):
         out_ref = refs[-1]
-        mixed = received_ref[...].astype(F32) + sign_ref[0, 0] * own_ref[...].astype(F32)
-        turned = jnp.dot(mixed.astype(BF), table_ref[...], preferred_element_type=F32)
-        out_ref[...] = (turned * scale).astype(BF)
+        for at in range(0, size, HB):
+            run = slice(at, at + HB)
+            mixed = received_ref[:, run].astype(F32) + sign_ref[0, 0] * own_ref[:, run].astype(F32)
+            turned = jnp.dot(mixed.astype(BF), table_ref[...], preferred_element_type=F32)
+            out_ref[:, run] = (turned * scale).astype(BF)
 
     args = [sign, own, received, table]
     specs = [
         SIGN_SPEC,
-        pl.BlockSpec((rows, HB), lambda i: (0, i)),
-        pl.BlockSpec((rows, HB), lambda i: (0, i)),
+        pl.BlockSpec((rows, size), lambda i: (0, i)),
+        pl.BlockSpec((rows, size), lambda i: (0, i)),
         pl.BlockSpec((HB, HB), lambda i: (0, 0)),
     ]
     aliases = None
@@ -133,10 +144,11 @@
         specs.append(pl.BlockSpec(memory_space=pl.ANY))
         aliases = {4: 0}
     return call(
-        kernel,
-        (blocks,),
+        "finish_grad",
+        kernel,
+        (steps,),
         specs,
-        pl.BlockSpec((rows, HB), lambda i: (0, first + i)),
+        pl.BlockSpec((rows, size), lambda i: (0, start + i)),
         jax.ShapeDtypeStruct((rows, total), BF),
         2 * rows * width * HB,
         6 * rows * width,
@@ -147,6 +159,7 @@
 def rotated_grad_parts(grads, weight, first, blocks, count):
     tokens, columns = grads.shape
     rows = tokens // count
+    steps, size, start = steps_for(first, blocks, 2, 256)
 
     def kernel(grads_ref, weight_ref, *out_refs):
         total = lax.dot_general(
@@ -156,13 +169,14 @@
             out_ref[...] = total[n * rows : (n + 1) * rows]
 
     return call(
-        kernel,
-        (blocks,),
+        "rotated_grad",
+        kernel,
+        (steps,),
         [
             pl.BlockSpec((tokens, columns), lambda i: (0, 0)),
-            pl.BlockSpec((HB, columns), lambda i: (first + i, 0)),
+            pl.BlockSpec((size, columns), lambda i: (start + i, 0)),
         ],
-        [pl.BlockSpec((rows, HB), lambda i: (0, i))] * count,
+        [pl.BlockSpec((rows, size), lambda i: (0, i))] * count,
         [jax.ShapeDtypeStruct((rows, blocks * HB), BF)] * count,
         2 * tokens * columns * blocks * HB,
         2 * blocks * HB * columns,
@@ -172,7 +186,7 @@
 def output_part(turned, weight, first, running, last):
     width, tokens = turned.shape
     columns = weight.shape[1]
-    blocks = width // HB
+    steps, size, start = steps_for(first, width // HB, 2, 256)
 
     def kernel(turned_ref, weight_ref, *refs):
         total_ref = refs[-1]
@@ -190,22 +204,23 @@
             turned_ref[...], weight_ref[...], (((0,), (0,)), ((), ())), preferred_element_type=F32
         )
 
-        @pl.when(step == blocks - 1)
+        @pl.when(step == steps - 1)
         def _():
             out_ref[...] = total_ref[...].astype(out_ref.dtype)
 
     whole = pl.BlockSpec((tokens, columns), lambda i: (0, 0))
     args = [turned, weight]
     specs = [
-        pl.BlockSpec((HB, tokens), lambda i: (i, 0)),
-        pl.BlockSpec((HB, columns), lambda i: (first + i, 0)),
+        pl.BlockSpec((size, tokens), lambda i: (i, 0)),
+        pl.BlockSpec((size, columns), lambda i: (start + i, 0)),
     ]
     if running is not None:
         args.append(running)
         specs.append(whole)
     return call(
-        kernel,
-        (blocks,),
+        "output",
+        kernel,
+        (steps,),
         specs,
         whole,
         jax.ShapeDtypeStruct((tokens, columns), BF if last else F32),
@@ -218,7 +233,7 @@
 def weight_grad_part(turned, grads, scale, first, total, result):
     width = turned[0].shape[0]
     columns = grads[0].shape[1]
-    blocks = width // HB
+    steps, size, start = steps_for(first, width // HB, 2, 256)
     count = len(turned)
     tokens = sum(piece.shape[1] for piece in turned)
 
@@ -230,7 +245,7 @@
         out_ref[...] = (product * scale).astype(BF)
 
     args = list(turned) + list(grads)
-    specs = [pl.BlockSpec((HB, piece.shape[1]), lambda i: (i, 0)) for piece in turned]
+    specs = [pl.BlockSpec((size, piece.shape[1]), lambda i: (i, 0)) for piece in turned]
     specs += [pl.BlockSpec(piece.shape, lambda i: (0, 0)) for piece in grads]
     aliases = None
     if result is not None:
@@ -238,10 +253,11 @@
         specs.append(pl.BlockSpec(memory_space=pl.ANY))
         aliases = {2 * count: 0}
     return call(
-        kernel,
-        (blocks,),
+        "weight_grad",
+        kernel,
+        (steps,),
         specs,
-        pl.BlockSpec((HB, columns), lambda i: (first + i, 0)),
+        pl.BlockSpec((size, columns), lambda i: (start + i, 0)),
         jax.ShapeDtypeStruct((total, columns), BF),
         2 * tokens * width * columns,
         2 * width * (columns + tokens),
@@ -250,11 +266,11 @@
 
 
 ORDER = [
-    "G", "h1", "G", "h1", "h2", "G", "h0", "g1", "g0", "h2", "h1", "G",
-    "g1", "g3", "h3", "h0", "h1", "h2", "h1", "g3", "h3", "g2", "g0", "h0",
-    "h1", "g1", "g2", "G", "h3", "h1", "h2", "g3", "h2", "g1", "h0", "h3",
-    "h0", "g2", "h3", "h2", "g3", "g0", "out", "h0", "g2", "h2", "h3", "h0",
-    "out", "g0", "h3", "out",
+    "h3", "G", "G", "h0", "h2", "G", "h2", "g3", "g0", "h0", "h1", "g1",
+    "h2", "g3", "G", "g0", "g2", "h3", "g3", "h1", "h2", "G", "g2", "h3",
+    "g1", "h2", "h3", "h0", "h3", "h1", "h2", "g3", "h1", "g0", "g1", "h0",
+    "h1", "h0", "g2", "h1", "h2", "out", "g1", "h0", "g0", "h1", "h0", "h3",
+    "g2", "out", "h3", "out",
 ]
 
 
@@ -323,13 +339,11 @@
         state["grad_pieces"] = pieces
 
     def hidden_part(first, size):
-        own, own_block = hidden, first
         sent = tied(hidden)[:, first * HB : (first + size) * HB]
         for bit in far_first[:-1]:
             arrived = send(sent, "tensor", bit)
             yield
-            own = done(combine(signs[bit], tied(own), own_block, arrived))
-            sent, own_block = own, 0
+            sent = done(combine(signs[bit], tied(sent), arrived))
         arrived = send(sent, "tensor", far_first[-1])
         yield
         turned = done(finish_hidden(signs[far_first[-1]], tied(sent), arrived, table, norm_scale))
@@ -368,13 +382,13 @@
             arrived = [send(term, "seq", bit) for term in terms[half:]]
             yield
             terms = [
-                done(combine(plus, tied(terms[n]), 0, arrived[n])) for n in range(half)
+                done(combine(plus, tied(terms[n]), arrived[n])) for n in range(half)
             ]
         own = terms[0]
         for bit in near_first[:-1]:
             arrived = send(own, "tensor", bit)
             yield
-            own = done(combine(signs[bit], tied(own), 0, arrived))
+            own = done(combine(signs[bit], tied(own), arrived))
         arrived = send(own, "tensor", near_first[-1])
         yield
         state["grad_hidden"] = done(

time: 284 us -> 259 us (0.912)
  Pallas kernels: 117 us -> 95.2 us
  waiting for transfers between devices: 105 us -> 85.9 us
  starting transfers between devices: 46.2 us -> 56.8 us
  local copies, waits for them, and re-layouts: 12 us -> 16.3 us
    pallas_call x32, Pallas kernels: 117 us -> 95.2 us  [the longest x4 43.3 us: weight_grad_part(): call('weight_grad', kernel, (steps,), specs, pl.BlockSpec((size, columns)...]
    ppermute x43, waiting for transfers between devices: 105 us -> 85.9 us  [partner(): lax.ppermute(shard, axis, [(i, i ^ 1 << bit) for i in range(lax.axis_size...]
    ppermute x43, starting transfers between devices: 46.2 us -> 56.8 us  [partner(): lax.ppermute(shard, axis, [(i, i ^ 1 << bit) for i in range(lax.axis_size...]
    unnamed x35 -> x45, local copies, waits for them, and re-layouts: 6.46 us -> 8.1 us
  transfers between devices with their start and end apart: 43 -> 43, of which waited for: 17 -> 14; matrix products, arithmetic and copies ran while one was open for 3% -> 5% of each run, Pallas kernels for 41% -> 37%
where the time goes in v2:
time: 259 us; the launch traced here: 258 us
  Pallas kernels  95.2 us (37%)
  waiting for transfers between devices  85.9 us (33%)
  starting transfers between devices  56.8 us (22%)
  local copies, waits for them, and re-layouts  16.3 us (6%)
  other arithmetic  3.06 us (1%)
    ppermute x43, waiting for transfers between devices, partner(): lax.ppermute(shard, axis, [(i, i ^ 1 << bit) for i in range(lax.axis_size...  85.9 us
    ppermute x43, starting transfers between devices, partner(): lax.ppermute(shard, axis, [(i, i ^ 1 << bit) for i in range(lax.axis_size...  56.8 us
    pallas_call x4, Pallas kernels, weight_grad_part(): call('weight_grad', kernel, (steps,), specs, pl.BlockSpec((size, columns)...  43.3 us
    pallas_call x4, Pallas kernels, output_part(): call('output', kernel, (steps,), specs, whole, jax.ShapeDtypeStruct((toke...  18.9 us
    pallas_call x4, Pallas kernels, rotated_grad_parts(): call('rotated_grad', kernel, (steps,), [pl.BlockSpec((tokens, columns), l...  18.3 us
    unnamed x45, local copies, waits for them, and re-layouts  8.1 us
    pallas_call x4, Pallas kernels, finish_grad(): call('finish_grad', kernel, (steps,), specs, pl.BlockSpec((rows, size), l...  6.12 us
  transfers between devices with their start and end apart: 43, of which 14 were waited for; matrix products, arithmetic and copies ran while one was open for 5% of the time, Pallas kernels for 37%

profile of v2, /device:TPU:0, one launch (start us, length us, event | category | flops | bytes accessed | tf_op | source)
XLA Modules:
  0.0 258.4 jit_solution(2390672297008129556)
XLA Ops:
  0.6 4.1 %collective-permute-start = (bf16[64,2048]{1,0:T(8,128)(2,1)}, bf16[64,2048]{1,0:T(8,128)(2,1)S(1)}, u32[]{:S(2)}, u32[]{:S(2)}) collective-permute-start(bf16[64,2048]{1,0:T(8,128)(2,1)} %param.5), channel_id=1, source_target_pairs={{0,2},{1,3},{2,0},{3,1},{4,6},{5,7},{6,4},{7,5},{8,10},{9,11},{10,... | collective-permute-start | bytes 786440 | tf_op jit(solution)/shard_map/ppermute | solution.py:18
  5.7 11.1 %collective-permute-done = bf16[64,2048]{1,0:T(8,128)(2,1)S(1)} collective-permute-done((bf16[64,2048]{1,0:T(8,128)(2,1)}, bf16[64,2048]{1,0:T(8,128)(2,1)S(1)}, u32[]{:S(2)}, u32[]{:S(2)}) %collective-permute-start) | collective-permute-done | bytes 262176 | tf_op jit(solution)/shard_map/ppermute | solution.py:18
  18.9 3.3 %collective-permute-start.2 = (bf16[128,2048]{1,0:T(8,128)(2,1)S(1)}, bf16[128,2048]{1,0:T(8,128)(2,1)S(1)}, u32[]{:S(2)}, u32[]{:S(2)}) collective-permute-start(bf16[128,2048]{1,0:T(8,128)(2,1)S(1)} %slice.19.own_ref), channel_id=1, source_target_pairs={{0,2},{1,3},{2,0},{3,1},{4,6},{5,7},{6,4},{7,5},{8,10},{9,11},{10,... | collective-permute-start | bytes 1572872 | tf_op jit(solution)/shard_map/ppermute | solution.py:18
  22.2 17.7 %collective-permute-done.1 = bf16[128,2048]{1,0:T(8,128)(2,1)S(1)} collective-permute-done((bf16[128,2048]{1,0:T(8,128)(2,1)S(1)}, bf16[128,2048]{1,0:T(8,128)(2,1)S(1)}, u32[]{:S(2)}, u32[]{:S(2)}) %collective-permute-start.1) | collective-permute-done | bytes 524320 | tf_op jit(solution)/shard_map/ppermute | solution.py:18
  43.7 10.0 %collective-permute-done.2.received_ref = bf16[128,2048]{1,0:T(8,128)(2,1)S(1)} collective-permute-done((bf16[128,2048]{1,0:T(8,128)(2,1)S(1)}, bf16[128,2048]{1,0:T(8,128)(2,1)S(1)}, u32[]{:S(2)}, u32[]{:S(2)}) %collective-permute-start.2) | collective-permute-done | bytes 524320 | tf_op jit(solution)/shard_map/ppermute | solution.py:18
  55.8 5.5 %rotated_grad.4 = (bf16[128,2048]{1,0:T(8,128)(2,1)S(1)}, bf16[128,2048]{1,0:T(8,128)(2,1)}) custom-call(bf16[256,2048]{1,0:T(8,128)(2,1)S(1)} %pad_maximum_fusion.1.grads_ref.refs_4_, bf16[7168,2048]{1,0:T(8,128)(2,1)} %weight_ref.15), custom_call_target="tpu_custom_call" | custom-call | flops 2147483648 | bytes 8388608 | tf_op jit(solution)/shard_map/rotated_grad/pallas_call | solution.py:171
  65.5 2.7 %collective-permute-start.6 = (bf16[128,2048]{1,0:T(8,128)(2,1)}, bf16[128,2048]{1,0:T(8,128)(2,1)}, u32[]{:S(2)}, u32[]{:S(2)}) collective-permute-start(bf16[128,2048]{1,0:T(8,128)(2,1)} %slice.20.own_ref), channel_id=1, source_target_pairs={{0,2},{1,3},{2,0},{3,1},{4,6},{5,7},{6,4},{7,5},{8,10},{9,11},{10,... | collective-permute-start | bytes 1572872 | tf_op jit(solution)/shard_map/ppermute | solution.py:18
  68.2 4.0 %rotated_grad.5 = (bf16[128,1536]{1,0:T(8,128)(2,1)S(1)}, bf16[128,1536]{1,0:T(8,128)(2,1)S(1)}) custom-call(bf16[256,2048]{1,0:T(8,128)(2,1)S(1)} %pad_maximum_fusion.1.grads_ref.refs_4_, bf16[7168,2048]{1,0:T(8,128)(2,1)} %weight_ref.15), custom_call_target="tpu_custom_call" | custom-call | flops 1610612736 | bytes 6291456 | tf_op jit(solution)/shard_map/rotated_grad/pallas_call | solution.py:171
  73.9 4.0 %rotated_grad.7 = (bf16[128,1536]{1,0:T(8,128)(2,1)S(1)}, bf16[128,1536]{1,0:T(8,128)(2,1)S(1)}) custom-call(bf16[256,2048]{1,0:T(8,128)(2,1)S(1)} %pad_maximum_fusion.1.grads_ref.refs_4_, bf16[7168,2048]{1,0:T(8,128)(2,1)} %weight_ref.15), custom_call_target="tpu_custom_call" | custom-call | flops 1610612736 | bytes 6291456 | tf_op jit(solution)/shard_map/rotated_grad/pallas_call | solution.py:171
  82.2 2.2 collective-permute-start.13
  84.5 4.8 %rotated_grad.6 = (bf16[128,2048]{1,0:T(8,128)(2,1)S(1)}, bf16[128,2048]{1,0:T(8,128)(2,1)S(1)}) custom-call(bf16[256,2048]{1,0:T(8,128)(2,1)S(1)} %pad_maximum_fusion.1.grads_ref.refs_4_, bf16[7168,2048]{1,0:T(8,128)(2,1)} %weight_ref.15), custom_call_target="tpu_custom_call" | custom-call | flops 2147483648 | bytes 8388608 | tf_op jit(solution)/shard_map/rotated_grad/pallas_call | solution.py:171
  92.4 12.0 %collective-permute-done.12.received_ref = bf16[128,2048]{1,0:T(8,128)(2,1)S(1)} collective-permute-done((bf16[128,2048]{1,0:T(8,128)(2,1)S(1)}, bf16[128,2048]{1,0:T(8,128)(2,1)S(1)}, u32[]{:S(2)}, u32[]{:S(2)}) %collective-permute-start.12) | collective-permute-done | bytes 524320 | tf_op jit(solution)/shard_map/ppermute | solution.py:18
  109.2 6.5 %collective-permute-done.9.received_ref = bf16[128,2048]{1,0:T(8,128)(2,1)S(1)} collective-permute-done((bf16[128,2048]{1,0:T(8,128)(2,1)S(1)}, bf16[128,2048]{1,0:T(8,128)(2,1)S(1)}, u32[]{:S(2)}, u32[]{:S(2)}) %collective-permute-start.9) | collective-permute-done | bytes 524320 | tf_op jit(solution)/shard_map/ppermute | solution.py:18
  116.9 2.3 collective-permute-done.14
  120.8 6.8 %collective-permute-done.15.received_ref = bf16[128,1536]{1,0:T(8,128)(2,1)S(1)} collective-permute-done((bf16[128,1536]{1,0:T(8,128)(2,1)S(1)}, bf16[128,1536]{1,0:T(8,128)(2,1)S(1)}, u32[]{:S(2)}, u32[]{:S(2)}) %collective-permute-start.15) | collective-permute-done | bytes 393248 | tf_op jit(solution)/shard_map/ppermute | solution.py:18
  127.6 7.3 %collective-permute-start.26 = (bf16[2048,256]{1,0:T(8,128)(2,1)S(1)}, bf16[2048,256]{1,0:T(8,128)(2,1)S(1)}, u32[]{:S(2)}, u32[]{:S(2)}) collective-permute-start(bf16[2048,256]{1,0:T(8,128)(2,1)S(1)} %constant_dynamic-update-slice_fusion.2.turned_ref.refs_0_), channel_id=1, source_target_pairs={{0,16},{8,24},{16,0},{24,8},{1,17},{9,25},{17,1},{25,9},{2,18},{10... | collective-permute-start | bytes 3145736 | tf_op jit(solution)/shard_map/ppermute | solution.py:18
  135.0 5.1 %output.4.refs_0_ = f32[256,2048]{1,0:T(8,128)S(1)} custom-call(bf16[2048,256]{1,0:T(8,128)(2,1)S(1)} %constant_dynamic-update-slice_fusion.2.turned_ref.refs_0_, bf16[7168,2048]{1,0:T(8,128)(2,1)} %weight_ref.15), custom_call_target="tpu_custom_call" | custom-call | flops 2147483648 | bytes 8388608 | tf_op jit(solution)/shard_map/output/pallas_call | solution.py:220
  142.5 5.3 %output.5.refs_0_ = f32[256,2048]{1,0:T(8,128)S(1)} custom-call(bf16[2048,256]{1,0:T(8,128)(2,1)} %constant_dynamic-update-slice_fusion.4.turned_ref.refs_0_, bf16[7168,2048]{1,0:T(8,128)(2,1)} %weight_ref.15, f32[256,2048]{1,0:T(8,128)S(1)} %output.4.refs_0_), custom_call_target="tpu_custom_call" | custom-call | flops 2147483648 | bytes 8388608 | tf_op jit(solution)/shard_map/output/pallas_call | solution.py:220
  152.4 4.1 %collective-permute-done.26.refs_1_ = bf16[2048,256]{1,0:T(8,128)(2,1)S(1)} collective-permute-done((bf16[2048,256]{1,0:T(8,128)(2,1)S(1)}, bf16[2048,256]{1,0:T(8,128)(2,1)S(1)}, u32[]{:S(2)}, u32[]{:S(2)}) %collective-permute-start.26) | collective-permute-done | bytes 1048608 | tf_op jit(solution)/shard_map/ppermute | solution.py:18
  157.2 3.2 %collective-permute-done.20 = bf16[1536,128]{1,0:T(8,128)(2,1)S(1)} collective-permute-done((bf16[1536,128]{1,0:T(8,128)(2,1)S(1)}, bf16[1536,128]{1,0:T(8,128)(2,1)S(1)}, u32[]{:S(2)}, u32[]{:S(2)}) %collective-permute-start.20) | collective-permute-done | bytes 393248 | tf_op jit(solution)/shard_map/ppermute | solution.py:18
  162.4 5.7 %collective-permute-start.32 = (bf16[1536,256]{1,0:T(8,128)(2,1)S(1)}, bf16[1536,256]{1,0:T(8,128)(2,1)}, u32[]{:S(2)}, u32[]{:S(2)}) collective-permute-start(bf16[1536,256]{1,0:T(8,128)(2,1)S(1)} %constant_dynamic-update-slice_fusion.6.turned_ref.refs_0_), channel_id=1, source_target_pairs={{0,16},{8,24},{16,0},{24,8},{1,17},{9,25},{17,1},{25,9},{2,18},{10... | collective-permute-start | bytes 2359304 | tf_op jit(solution)/shard_map/ppermute | solution.py:18
  168.9 2.3 collective-permute-start.30
  173.9 7.4 %collective-permute-start.35 = (bf16[1536,256]{1,0:T(8,128)(2,1)}, bf16[1536,256]{1,0:T(8,128)(2,1)}, u32[]{:S(2)}, u32[]{:S(2)}) collective-permute-start(bf16[1536,256]{1,0:T(8,128)(2,1)} %constant_dynamic-update-slice_fusion.8.turned_ref.refs_0_), channel_id=1, source_target_pairs={{0,16},{8,24},{16,0},{24,8},{1,17},{9,25},{17,1},{25,9},{2,18},{10... | collective-permute-start | bytes 2359304 | tf_op jit(solution)/shard_map/ppermute | solution.py:18
  181.4 4.2 %output.6.refs_0_ = f32[256,2048]{1,0:T(8,128)S(1)} custom-call(bf16[1536,256]{1,0:T(8,128)(2,1)S(1)} %constant_dynamic-update-slice_fusion.6.turned_ref.refs_0_, bf16[7168,2048]{1,0:T(8,128)(2,1)} %weight_ref.15, f32[256,2048]{1,0:T(8,128)S(1)} %output.5.refs_0_), custom_call_target="tpu_custom_call" | custom-call | flops 1610612736 | bytes 6291456 | tf_op jit(solution)/shard_map/output/pallas_call | solution.py:220
  185.6 4.3 %output.7 = bf16[256,2048]{1,0:T(8,128)(2,1)S(1)} custom-call(bf16[1536,256]{1,0:T(8,128)(2,1)} %constant_dynamic-update-slice_fusion.8.turned_ref.refs_0_, bf16[7168,2048]{1,0:T(8,128)(2,1)} %weight_ref.15, f32[256,2048]{1,0:T(8,128)S(1)} %output.6.refs_0_), custom_call_target="tpu_custom_call" | custom-call | flops 1610612736 | bytes 6291456 | tf_op jit(solution)/shard_map/output/pallas_call | solution.py:220
  193.1 11.0 %weight_grad.4.refs_8_ = bf16[7168,2048]{1,0:T(8,128)(2,1)} custom-call(bf16[2048,256]{1,0:T(8,128)(2,1)S(1)} %constant_dynamic-update-slice_fusion.2.turned_ref.refs_0_, bf16[2048,256]{1,0:T(8,128)(2,1)S(1)} %collective-permute-done.26.refs_1_, bf16[2048,256]{1,0:T(8,128)(2,1)S(1)} %collective-permute-done.27.refs_2_, ...), custom_call_target="tpu_custom_call" | custom-call | flops 85899344 | bytes 125829 | tf_op jit(solution)/shard_map/weight_grad/pallas_call | solution.py:255
  205.6 6.2 %collective-permute-done.31.received_ref = bf16[128,1536]{1,0:T(8,128)(2,1)S(1)} collective-permute-done((bf16[128,1536]{1,0:T(8,128)(2,1)S(1)}, bf16[128,1536]{1,0:T(8,128)(2,1)S(1)}, u32[]{:S(2)}, u32[]{:S(2)}) %collective-permute-start.31) | collective-permute-done | bytes 393248 | tf_op jit(solution)/shard_map/ppermute | solution.py:18
  214.7 2.7 %collective-permute-start.24 = (bf16[128,2048]{1,0:T(8,128)(2,1)}, bf16[128,2048]{1,0:T(8,128)(2,1)}, u32[]{:S(2)}, u32[]{:S(2)}) collective-permute-start(bf16[128,2048]{1,0:T(8,128)(2,1)} %pad_maximum_fusion.2), channel_id=1, source_target_pairs={{0,1},{1,0},{2,3},{3,2},{4,5},{5,4},{6,7},{7,6},{8,9},{9,8},{10,11... | collective-permute-start | bytes 1572872 | tf_op jit(solution)/shard_map/ppermute | solution.py:18
  218.6 9.8 %weight_grad.5.refs_8_ = bf16[7168,2048]{1,0:T(8,128)(2,1)} custom-call(bf16[1536,256]{1,0:T(8,128)(2,1)S(1)} %constant_dynamic-update-slice_fusion.6.turned_ref.refs_0_, bf16[1536,256]{1,0:T(8,128)(2,1)} %collective-permute-done.32.refs_1_, bf16[1536,256]{1,0:T(8,128)(2,1)} %collective-permute-done.33.refs_2_, ...), custom_call_target="tpu_custom_call", output_to_operand_aliasing={{}: (8, {})} | custom-call | flops 64424508 | bytes 94371 | tf_op jit(solution)/shard_map/weight_grad/pallas_call | solution.py:255
  228.3 10.0 %weight_grad.6.refs_8_ = bf16[7168,2048]{1,0:T(8,128)(2,1)} custom-call(bf16[1536,256]{1,0:T(8,128)(2,1)} %constant_dynamic-update-slice_fusion.8.turned_ref.refs_0_, bf16[1536,256]{1,0:T(8,128)(2,1)} %collective-permute-done.35.refs_1_, bf16[1536,256]{1,0:T(8,128)(2,1)} %collective-permute-done.36.refs_2_, ...), custom_call_target="tpu_custom_call", output_to_operand_aliasing={{}: (8, {})} | custom-call | flops 64424508 | bytes 94371 | tf_op jit(solution)/shard_map/weight_grad/pallas_call | solution.py:255
  240.2 2.4 finish_grad.7
  244.0 12.6 %weight_grad.7 = bf16[7168,2048]{1,0:T(8,128)(2,1)} custom-call(bf16[2048,256]{1,0:T(8,128)(2,1)} %constant_dynamic-update-slice_fusion.4.turned_ref.refs_0_, bf16[2048,256]{1,0:T(8,128)(2,1)} %collective-permute-done.40.refs_1_, bf16[2048,256]{1,0:T(8,128)(2,1)} %collective-permute-done.41.refs_2_, ...), custom_call_target="tpu_custom_call", output_to_operand_aliasing={{}: (8, {})} | custom-call | flops 85899344 | bytes 125829 | tf_op jit(solution)/shard_map/weight_grad/pallas_call | solution.py:255
  (147 shorter events, 56.7 us)
Async XLA Ops:
  16.9 23.0 %collective-permute-start.1 = (bf16[128,2048]{1,0:T(8,128)(2,1)S(1)}, bf16[128,2048]{1,0:T(8,128)(2,1)S(1)}, u32[]{:S(2)}, u32[]{:S(2)}) collective-permute-start(bf16[128,2048]{1,0:T(8,128)(2,1)S(1)} %constant_dynamic-update-slice_fusion), channel_id=1, source_target_pairs={{0,1},{1,0},{2,3},{3,2},{4,5},{5,4},{6,7},{7,6},{8,9},{9,8},{10,11... | collective-permute-start | bytes 1572872 | tf_op jit(solution)/shard_map/ppermute | solution.py:18
  18.9 34.8 %collective-permute-start.2 = (bf16[128,2048]{1,0:T(8,128)(2,1)S(1)}, bf16[128,2048]{1,0:T(8,128)(2,1)S(1)}, u32[]{:S(2)}, u32[]{:S(2)}) collective-permute-start(bf16[128,2048]{1,0:T(8,128)(2,1)S(1)} %slice.19.own_ref), channel_id=1, source_target_pairs={{0,2},{1,3},{2,0},{3,1},{4,6},{5,7},{6,4},{7,5},{8,10},{9,11},{10,... | collective-permute-start | bytes 1572872 | tf_op jit(solution)/shard_map/ppermute | solution.py:18
  40.3 37.7 %collective-permute-start.4 = (bf16[256,2048]{1,0:T(8,128)(2,1)S(1)}, bf16[256,2048]{1,0:T(8,128)(2,1)S(1)}, u32[]{:S(2)}, u32[]{:S(2)}) collective-permute-start(bf16[256,2048]{1,0:T(8,128)(2,1)S(1)} %pad_maximum_fusion.1.grads_ref.refs_4_), channel_id=1, source_target_pairs={{0,16},{8,24},{16,0},{24,8},{1,17},{9,25},{17,1},{25,9},{2,18},{10... | collective-permute-start | bytes 3145736 | tf_op jit(solution)/shard_map/ppermute | solution.py:18
  42.7 29.5 %collective-permute-start.3 = (bf16[128,1536]{1,0:T(8,128)(2,1)S(1)}, bf16[128,1536]{1,0:T(8,128)(2,1)}, u32[]{:S(2)}, u32[]{:S(2)}) collective-permute-start(bf16[128,1536]{1,0:T(8,128)(2,1)S(1)} %slice.18.own_ref), channel_id=1, source_target_pairs={{0,2},{1,3},{2,0},{3,1},{4,6},{5,7},{6,4},{7,5},{8,10},{9,11},{10,... | collective-permute-start | bytes 1179656 | tf_op jit(solution)/shard_map/ppermute | solution.py:18
  55.7 22.3 %collective-permute-start.10 = (bf16[128,2048]{1,0:T(8,128)(2,1)S(1)}, bf16[128,2048]{1,0:T(8,128)(2,1)}, u32[]{:S(2)}, u32[]{:S(2)}) collective-permute-start(bf16[128,2048]{1,0:T(8,128)(2,1)S(1)} %combine.12.own_ref), channel_id=1, source_target_pairs={{0,1},{1,0},{2,3},{3,2},{4,5},{5,4},{6,7},{7,6},{8,9},{9,8},{10,11... | collective-permute-start | bytes 1572872 | tf_op jit(solution)/shard_map/ppermute | solution.py:18
  62.1 17.7 %collective-permute-start.11 = (bf16[128,2048]{1,0:T(8,128)(2,1)}, bf16[128,2048]{1,0:T(8,128)(2,1)}, u32[]{:S(2)}, u32[]{:S(2)}) collective-permute-start(bf16[128,2048]{1,0:T(8,128)(2,1)} %get-tuple-element.118), channel_id=1, source_target_pairs={{0,4},{4,0},{1,5},{5,1},{2,6},{6,2},{3,7},{7,3},{8,12},{12,8},{9,1... | collective-permute-start | bytes 1572872 | tf_op jit(solution)/shard_map/ppermute | solution.py:18
  65.5 25.5 %collective-permute-start.6 = (bf16[128,2048]{1,0:T(8,128)(2,1)}, bf16[128,2048]{1,0:T(8,128)(2,1)}, u32[]{:S(2)}, u32[]{:S(2)}) collective-permute-start(bf16[128,2048]{1,0:T(8,128)(2,1)} %slice.20.own_ref), channel_id=1, source_target_pairs={{0,2},{1,3},{2,0},{3,1},{4,6},{5,7},{6,4},{7,5},{8,10},{9,11},{10,... | collective-permute-start | bytes 1572872 | tf_op jit(solution)/shard_map/ppermute | solution.py:18
  77.9 28.9 %collective-permute-start.7 = (bf16[256,2048]{1,0:T(8,128)(2,1)S(1)}, bf16[256,2048]{1,0:T(8,128)(2,1)S(1)}, u32[]{:S(2)}, u32[]{:S(2)}) collective-permute-start(bf16[256,2048]{1,0:T(8,128)(2,1)S(1)} %collective-permute-done.4.refs_5_), channel_id=1, source_target_pairs={{0,8},{8,0},{16,24},{24,16},{1,9},{9,1},{17,25},{25,17},{2,10},{10... | collective-permute-start | bytes 3145736 | tf_op jit(solution)/shard_map/ppermute | solution.py:18
  81.1 23.3 %collective-permute-start.12 = (bf16[128,2048]{1,0:T(8,128)(2,1)S(1)}, bf16[128,2048]{1,0:T(8,128)(2,1)S(1)}, u32[]{:S(2)}, u32[]{:S(2)}) collective-permute-start(bf16[128,2048]{1,0:T(8,128)(2,1)S(1)} %combine.17.own_ref), channel_id=1, source_target_pairs={{0,1},{1,0},{2,3},{3,2},{4,5},{5,4},{6,7},{7,6},{8,9},{9,8},{10,11... | collective-permute-start | bytes 1572872 | tf_op jit(solution)/shard_map/ppermute | solution.py:18
  82.2 23.9 %collective-permute-start.13 = (bf16[128,1536]{1,0:T(8,128)(2,1)S(1)}, bf16[128,1536]{1,0:T(8,128)(2,1)S(1)}, u32[]{:S(2)}, u32[]{:S(2)}) collective-permute-start(bf16[128,1536]{1,0:T(8,128)(2,1)S(1)} %slice.21.own_ref), channel_id=1, source_target_pairs={{0,2},{1,3},{2,0},{3,1},{4,6},{5,7},{6,4},{7,5},{8,10},{9,11},{10,... | collective-permute-start | bytes 1179656 | tf_op jit(solution)/shard_map/ppermute | solution.py:18
  89.4 17.6 %collective-permute-start.8 = (bf16[128,2048]{1,0:T(8,128)(2,1)S(1)}, bf16[128,2048]{1,0:T(8,128)(2,1)S(1)}, u32[]{:S(2)}, u32[]{:S(2)}) collective-permute-start(bf16[128,2048]{1,0:T(8,128)(2,1)S(1)} %get-tuple-element.108), channel_id=1, source_target_pairs={{0,4},{4,0},{1,5},{5,1},{2,6},{6,2},{3,7},{7,3},{8,12},{12,8},{9,1... | collective-permute-start | bytes 1572872 | tf_op jit(solution)/shard_map/ppermute | solution.py:18
  92.3 23.3 %collective-permute-start.9 = (bf16[128,2048]{1,0:T(8,128)(2,1)S(1)}, bf16[128,2048]{1,0:T(8,128)(2,1)S(1)}, u32[]{:S(2)}, u32[]{:S(2)}) collective-permute-start(bf16[128,2048]{1,0:T(8,128)(2,1)S(1)} %combine.15.own_ref), channel_id=1, source_target_pairs={{0,1},{1,0},{2,3},{3,2},{4,5},{5,4},{6,7},{7,6},{8,9},{9,8},{10,11... | collective-permute-start | bytes 1572872 | tf_op jit(solution)/shard_map/ppermute | solution.py:18
  106.1 21.5 %collective-permute-start.15 = (bf16[128,1536]{1,0:T(8,128)(2,1)S(1)}, bf16[128,1536]{1,0:T(8,128)(2,1)S(1)}, u32[]{:S(2)}, u32[]{:S(2)}) collective-permute-start(bf16[128,1536]{1,0:T(8,128)(2,1)S(1)} %get-tuple-element.127), channel_id=1, source_target_pairs={{0,4},{4,0},{1,5},{5,1},{2,6},{6,2},{3,7},{7,3},{8,12},{12,8},{9,1... | collective-permute-start | bytes 1179656 | tf_op jit(solution)/shard_map/ppermute | solution.py:18
  106.9 35.0 %collective-permute-start.17 = (bf16[128,1536]{1,0:T(8,128)(2,1)S(1)}, bf16[128,1536]{1,0:T(8,128)(2,1)S(1)}, u32[]{:S(2)}, u32[]{:S(2)}) collective-permute-start(bf16[128,1536]{1,0:T(8,128)(2,1)S(1)} %combine.13.own_ref), channel_id=1, source_target_pairs={{0,1},{1,0},{2,3},{3,2},{4,5},{5,4},{6,7},{7,6},{8,9},{9,8},{10,11... | collective-permute-start | bytes 1179656 | tf_op jit(solution)/shard_map/ppermute | solution.py:18
  107.0 40.8 %collective-permute-start.18 = (bf16[128,1536]{1,0:T(8,128)(2,1)S(1)}, bf16[128,1536]{1,0:T(8,128)(2,1)S(1)}, u32[]{:S(2)}, u32[]{:S(2)}) collective-permute-start(bf16[128,1536]{1,0:T(8,128)(2,1)S(1)} %combine.19.own_ref), channel_id=1, source_target_pairs={{0,1},{1,0},{2,3},{3,2},{4,5},{5,4},{6,7},{7,6},{8,9},{9,8},{10,11... | collective-permute-start | bytes 1179656 | tf_op jit(solution)/shard_map/ppermute | solution.py:18
  115.6 33.3 %collective-permute-start.19 = (bf16[128,2048]{1,0:T(8,128)(2,1)S(1)}, bf16[128,2048]{1,0:T(8,128)(2,1)S(1)}, u32[]{:S(2)}, u32[]{:S(2)}) collective-permute-start(bf16[128,2048]{1,0:T(8,128)(2,1)S(1)} %combine.18.own_ref), channel_id=1, source_target_pairs={{0,2},{1,3},{2,0},{3,1},{4,6},{5,7},{6,4},{7,5},{8,10},{9,11},{10,... | collective-permute-start | bytes 1572872 | tf_op jit(solution)/shard_map/ppermute | solution.py:18
  119.2 21.8 %collective-permute-start.16 = (bf16[2048,128]{1,0:T(8,128)(2,1)S(1)}, bf16[2048,128]{1,0:T(8,128)(2,1)S(1)}, u32[]{:S(2)}, u32[]{:S(2)}) collective-permute-start(bf16[2048,128]{1,0:T(8,128)(2,1)S(1)} %finish_hidden.4), channel_id=1, source_target_pairs={{0,4},{4,0},{1,5},{5,1},{2,6},{6,2},{3,7},{7,3},{8,12},{12,8},{9,1... | collective-permute-start | bytes 1572872 | tf_op jit(solution)/shard_map/ppermute | solution.py:18
  127.6 28.9 %collective-permute-start.26 = (bf16[2048,256]{1,0:T(8,128)(2,1)S(1)}, bf16[2048,256]{1,0:T(8,128)(2,1)S(1)}, u32[]{:S(2)}, u32[]{:S(2)}) collective-permute-start(bf16[2048,256]{1,0:T(8,128)(2,1)S(1)} %constant_dynamic-update-slice_fusion.2.turned_ref.refs_0_), channel_id=1, source_target_pairs={{0,16},{8,24},{16,0},{24,8},{1,17},{9,25},{17,1},{25,9},{2,18},{10... | collective-permute-start | bytes 3145736 | tf_op jit(solution)/shard_map/ppermute | solution.py:18
  141.0 21.4 %collective-permute-start.29 = (bf16[256,2048]{1,0:T(8,128)(2,1)S(1)}, bf16[256,2048]{1,0:T(8,128)(2,1)S(1)}, u32[]{:S(2)}, u32[]{:S(2)}) collective-permute-start(bf16[256,2048]{1,0:T(8,128)(2,1)S(1)} %pad_maximum_fusion.1.grads_ref.refs_4_), channel_id=1, source_target_pairs={{0,8},{8,0},{16,24},{24,16},{1,9},{9,1},{17,25},{25,17},{2,10},{10... | collective-permute-start | bytes 3145736 | tf_op jit(solution)/shard_map/ppermute | solution.py:18
  156.5 17.4 %collective-permute-start.25 = (bf16[128,2048]{1,0:T(8,128)(2,1)S(1)}, bf16[128,2048]{1,0:T(8,128)(2,1)S(1)}, u32[]{:S(2)}, u32[]{:S(2)}) collective-permute-start(bf16[128,2048]{1,0:T(8,128)(2,1)S(1)} %combine.16.own_ref), channel_id=1, source_target_pairs={{0,1},{1,0},{2,3},{3,2},{4,5},{5,4},{6,7},{7,6},{8,9},{9,8},{10,11... | collective-permute-start | bytes 1572872 | tf_op jit(solution)/shard_map/ppermute | solution.py:18
  160.3 31.6 %collective-permute-start.28 = (bf16[2048,256]{1,0:T(8,128)(2,1)S(1)}, bf16[2048,256]{1,0:T(8,128)(2,1)S(1)}, u32[]{:S(2)}, u32[]{:S(2)}) collective-permute-start(bf16[2048,256]{1,0:T(8,128)(2,1)S(1)} %collective-permute-done.26.refs_1_), channel_id=1, source_target_pairs={{0,8},{8,0},{16,24},{24,16},{1,9},{9,1},{17,25},{25,17},{2,10},{10... | collective-permute-start | bytes 3145736 | tf_op jit(solution)/shard_map/ppermute | solution.py:18
  162.2 30.7 %collective-permute-start.27 = (bf16[2048,256]{1,0:T(8,128)(2,1)S(1)}, bf16[2048,256]{1,0:T(8,128)(2,1)S(1)}, u32[]{:S(2)}, u32[]{:S(2)}) collective-permute-start(bf16[2048,256]{1,0:T(8,128)(2,1)S(1)} %constant_dynamic-update-slice_fusion.2.turned_ref.refs_0_), channel_id=1, source_target_pairs={{0,8},{8,0},{16,24},{24,16},{1,9},{9,1},{17,25},{25,17},{2,10},{10... | collective-permute-start | bytes 3145736 | tf_op jit(solution)/shard_map/ppermute | solution.py:18
  162.4 29.6 %collective-permute-start.32 = (bf16[1536,256]{1,0:T(8,128)(2,1)S(1)}, bf16[1536,256]{1,0:T(8,128)(2,1)}, u32[]{:S(2)}, u32[]{:S(2)}) collective-permute-start(bf16[1536,256]{1,0:T(8,128)(2,1)S(1)} %constant_dynamic-update-slice_fusion.6.turned_ref.refs_0_), channel_id=1, source_target_pairs={{0,16},{8,24},{16,0},{24,8},{1,17},{9,25},{17,1},{25,9},{2,18},{10... | collective-permute-start | bytes 2359304 | tf_op jit(solution)/shard_map/ppermute | solution.py:18
  168.9 23.0 %collective-permute-start.30 = (bf16[128,1536]{1,0:T(8,128)(2,1)S(1)}, bf16[128,1536]{1,0:T(8,128)(2,1)S(1)}, u32[]{:S(2)}, u32[]{:S(2)}) collective-permute-start(bf16[128,1536]{1,0:T(8,128)(2,1)S(1)} %combine.22.own_ref), channel_id=1, source_target_pairs={{0,2},{1,3},{2,0},{3,1},{4,6},{5,7},{6,4},{7,5},{8,10},{9,11},{10,... | collective-permute-start | bytes 1179656 | tf_op jit(solution)/shard_map/ppermute | solution.py:18
  173.9 31.4 %collective-permute-start.35 = (bf16[1536,256]{1,0:T(8,128)(2,1)}, bf16[1536,256]{1,0:T(8,128)(2,1)}, u32[]{:S(2)}, u32[]{:S(2)}) collective-permute-start(bf16[1536,256]{1,0:T(8,128)(2,1)} %constant_dynamic-update-slice_fusion.8.turned_ref.refs_0_), channel_id=1, source_target_pairs={{0,16},{8,24},{16,0},{24,8},{1,17},{9,25},{17,1},{25,9},{2,18},{10... | collective-permute-start | bytes 2359304 | tf_op jit(solution)/shard_map/ppermute | solution.py:18
  191.9 21.9 %collective-permute-start.33 = (bf16[1536,256]{1,0:T(8,128)(2,1)S(1)}, bf16[1536,256]{1,0:T(8,128)(2,1)}, u32[]{:S(2)}, u32[]{:S(2)}) collective-permute-start(bf16[1536,256]{1,0:T(8,128)(2,1)S(1)} %constant_dynamic-update-slice_fusion.6.turned_ref.refs_0_), channel_id=1, source_target_pairs={{0,8},{8,0},{16,24},{24,16},{1,9},{9,1},{17,25},{25,17},{2,10},{10... | collective-permute-start | bytes 2359304 | tf_op jit(solution)/shard_map/ppermute | solution.py:18
  191.9 19.9 %collective-permute-start.31 = (bf16[128,1536]{1,0:T(8,128)(2,1)S(1)}, bf16[128,1536]{1,0:T(8,128)(2,1)S(1)}, u32[]{:S(2)}, u32[]{:S(2)}) collective-permute-start(bf16[128,1536]{1,0:T(8,128)(2,1)S(1)} %combine.21.own_ref), channel_id=1, source_target_pairs={{0,2},{1,3},{2,0},{3,1},{4,6},{5,7},{6,4},{7,5},{8,10},{9,11},{10,... | collective-permute-start | bytes 1179656 | tf_op jit(solution)/shard_map/ppermute | solution.py:18
  192.0 46.3 %collective-permute-start.40 = (bf16[2048,256]{1,0:T(8,128)(2,1)}, bf16[2048,256]{1,0:T(8,128)(2,1)}, u32[]{:S(2)}, u32[]{:S(2)}) collective-permute-start(bf16[2048,256]{1,0:T(8,128)(2,1)} %constant_dynamic-update-slice_fusion.4.turned_ref.refs_0_), channel_id=1, source_target_pairs={{0,16},{8,24},{16,0},{24,8},{1,17},{9,25},{17,1},{25,9},{2,18},{10... | collective-permute-start | bytes 3145736 | tf_op jit(solution)/shard_map/ppermute | solution.py:18
  192.9 21.8 %collective-permute-start.34 = (bf16[1536,256]{1,0:T(8,128)(2,1)}, bf16[1536,256]{1,0:T(8,128)(2,1)}, u32[]{:S(2)}, u32[]{:S(2)}) collective-permute-start(bf16[1536,256]{1,0:T(8,128)(2,1)} %collective-permute-done.32.refs_1_), channel_id=1, source_target_pairs={{0,8},{8,0},{16,24},{24,16},{1,9},{9,1},{17,25},{25,17},{2,10},{10... | collective-permute-start | bytes 2359304 | tf_op jit(solution)/shard_map/ppermute | solution.py:18
  205.3 23.1 %collective-permute-start.36 = (bf16[1536,256]{1,0:T(8,128)(2,1)}, bf16[1536,256]{1,0:T(8,128)(2,1)}, u32[]{:S(2)}, u32[]{:S(2)}) collective-permute-start(bf16[1536,256]{1,0:T(8,128)(2,1)} %constant_dynamic-update-slice_fusion.8.turned_ref.refs_0_), channel_id=1, source_target_pairs={{0,8},{8,0},{16,24},{24,16},{1,9},{9,1},{17,25},{25,17},{2,10},{10... | collective-permute-start | bytes 2359304 | tf_op jit(solution)/shard_map/ppermute | solution.py:18
  213.8 26.4 %collective-permute-start.38 = (bf16[128,2048]{1,0:T(8,128)(2,1)}, bf16[128,2048]{1,0:T(8,128)(2,1)}, u32[]{:S(2)}, u32[]{:S(2)}) collective-permute-start(bf16[128,2048]{1,0:T(8,128)(2,1)} %copy-done.9), channel_id=1, source_target_pairs={{0,2},{1,3},{2,0},{3,1},{4,6},{5,7},{6,4},{7,5},{8,10},{9,11},{10,... | collective-permute-start | bytes 1572872 | tf_op jit(solution)/shard_map/ppermute | solution.py:18
  214.7 27.9 %collective-permute-start.24 = (bf16[128,2048]{1,0:T(8,128)(2,1)}, bf16[128,2048]{1,0:T(8,128)(2,1)}, u32[]{:S(2)}, u32[]{:S(2)}) collective-permute-start(bf16[128,2048]{1,0:T(8,128)(2,1)} %pad_maximum_fusion.2), channel_id=1, source_target_pairs={{0,1},{1,0},{2,3},{3,2},{4,5},{5,4},{6,7},{7,6},{8,9},{9,8},{10,11... | collective-permute-start | bytes 1572872 | tf_op jit(solution)/shard_map/ppermute | solution.py:18
  (31 other events, 372.8 us)

commit v3 on v2

--- a/solution.py
+++ b/solution.py
@@ -233,7 +233,7 @@
 def weight_grad_part(turned, grads, scale, first, total, result):
     width = turned[0].shape[0]
     columns = grads[0].shape[1]
-    steps, size, start = steps_for(first, width // HB, 2, 256)
+    steps, size, start = steps_for(first, width // HB, width // HB, 256)
     count = len(turned)
     tokens = sum(piece.shape[1] for piece in turned)
 

time: 259 us -> 259 us (level)
  transfers between devices with their start and end apart: 43 -> 43, of which waited for: 14 -> 14; matrix products, arithmetic and copies ran while one was open for 5% -> 5% of each run, Pallas kernels for 37% -> 36%
where the time goes in v3:
time: 259 us; the launch traced here: 258 us
  Pallas kernels  93.7 us (36%)
  waiting for transfers between devices  87.4 us (34%)
  starting transfers between devices  56.8 us (22%)
  local copies, waits for them, and re-layouts  16.3 us (6%)
  other arithmetic  3.06 us (1%)
    ppermute x43, waiting for transfers between devices, partner(): lax.ppermute(shard, axis, [(i, i ^ 1 << bit) for i in range(lax.axis_size...  87.4 us
    ppermute x43, starting transfers between devices, partner(): lax.ppermute(shard, axis, [(i, i ^ 1 << bit) for i in range(lax.axis_size...  56.8 us
    pallas_call x4, Pallas kernels, weight_grad_part(): call('weight_grad', kernel, (steps,), specs, pl.BlockSpec((size, columns)...  41.8 us
    pallas_call x4, Pallas kernels, output_part(): call('output', kernel, (steps,), specs, whole, jax.ShapeDtypeStruct((toke...  18.9 us
    pallas_call x4, Pallas kernels, rotated_grad_parts(): call('rotated_grad', kernel, (steps,), [pl.BlockSpec((tokens, columns), l...  18.3 us
    unnamed x45, local copies, waits for them, and re-layouts  8.1 us
    pallas_call x4, Pallas kernels, finish_grad(): call('finish_grad', kernel, (steps,), specs, pl.BlockSpec((rows, size), l...  6.11 us
  transfers between devices with their start and end apart: 43, of which 14 were waited for; matrix products, arithmetic and copies ran while one was open for 5% of the time, Pallas kernels for 36%

profile of v3, /device:TPU:0, one launch (start us, length us, event | category | flops | bytes accessed | tf_op | source)
XLA Modules:
  0.0 258.4 jit_solution(6420712335870865355)
XLA Ops:
  0.6 4.1 %collective-permute-start = (bf16[64,2048]{1,0:T(8,128)(2,1)}, bf16[64,2048]{1,0:T(8,128)(2,1)S(1)}, u32[]{:S(2)}, u32[]{:S(2)}) collective-permute-start(bf16[64,2048]{1,0:T(8,128)(2,1)} %param.5), channel_id=1, source_target_pairs={{0,2},{1,3},{2,0},{3,1},{4,6},{5,7},{6,4},{7,5},{8,10},{9,11},{10,... | collective-permute-start | bytes 786440 | tf_op jit(solution)/shard_map/ppermute | solution.py:18
  5.7 11.1 %collective-permute-done = bf16[64,2048]{1,0:T(8,128)(2,1)S(1)} collective-permute-done((bf16[64,2048]{1,0:T(8,128)(2,1)}, bf16[64,2048]{1,0:T(8,128)(2,1)S(1)}, u32[]{:S(2)}, u32[]{:S(2)}) %collective-permute-start) | collective-permute-done | bytes 262176 | tf_op jit(solution)/shard_map/ppermute | solution.py:18
  18.9 3.3 %collective-permute-start.2 = (bf16[128,2048]{1,0:T(8,128)(2,1)S(1)}, bf16[128,2048]{1,0:T(8,128)(2,1)S(1)}, u32[]{:S(2)}, u32[]{:S(2)}) collective-permute-start(bf16[128,2048]{1,0:T(8,128)(2,1)S(1)} %slice.19.own_ref), channel_id=1, source_target_pairs={{0,2},{1,3},{2,0},{3,1},{4,6},{5,7},{6,4},{7,5},{8,10},{9,11},{10,... | collective-permute-start | bytes 1572872 | tf_op jit(solution)/shard_map/ppermute | solution.py:18
  22.2 17.7 %collective-permute-done.1 = bf16[128,2048]{1,0:T(8,128)(2,1)S(1)} collective-permute-done((bf16[128,2048]{1,0:T(8,128)(2,1)S(1)}, bf16[128,2048]{1,0:T(8,128)(2,1)S(1)}, u32[]{:S(2)}, u32[]{:S(2)}) %collective-permute-start.1) | collective-permute-done | bytes 524320 | tf_op jit(solution)/shard_map/ppermute | solution.py:18
  43.7 10.0 %collective-permute-done.2.received_ref = bf16[128,2048]{1,0:T(8,128)(2,1)S(1)} collective-permute-done((bf16[128,2048]{1,0:T(8,128)(2,1)S(1)}, bf16[128,2048]{1,0:T(8,128)(2,1)S(1)}, u32[]{:S(2)}, u32[]{:S(2)}) %collective-permute-start.2) | collective-permute-done | bytes 524320 | tf_op jit(solution)/shard_map/ppermute | solution.py:18
  55.8 5.5 %rotated_grad.4 = (bf16[128,2048]{1,0:T(8,128)(2,1)S(1)}, bf16[128,2048]{1,0:T(8,128)(2,1)}) custom-call(bf16[256,2048]{1,0:T(8,128)(2,1)S(1)} %pad_maximum_fusion.1.grads_ref.refs_4_, bf16[7168,2048]{1,0:T(8,128)(2,1)} %weight_ref.15), custom_call_target="tpu_custom_call" | custom-call | flops 2147483648 | bytes 8388608 | tf_op jit(solution)/shard_map/rotated_grad/pallas_call | solution.py:171
  65.5 2.7 %collective-permute-start.6 = (bf16[128,2048]{1,0:T(8,128)(2,1)}, bf16[128,2048]{1,0:T(8,128)(2,1)}, u32[]{:S(2)}, u32[]{:S(2)}) collective-permute-start(bf16[128,2048]{1,0:T(8,128)(2,1)} %slice.20.own_ref), channel_id=1, source_target_pairs={{0,2},{1,3},{2,0},{3,1},{4,6},{5,7},{6,4},{7,5},{8,10},{9,11},{10,... | collective-permute-start | bytes 1572872 | tf_op jit(solution)/shard_map/ppermute | solution.py:18
  68.2 4.0 %rotated_grad.5 = (bf16[128,1536]{1,0:T(8,128)(2,1)S(1)}, bf16[128,1536]{1,0:T(8,128)(2,1)S(1)}) custom-call(bf16[256,2048]{1,0:T(8,128)(2,1)S(1)} %pad_maximum_fusion.1.grads_ref.refs_4_, bf16[7168,2048]{1,0:T(8,128)(2,1)} %weight_ref.15), custom_call_target="tpu_custom_call" | custom-call | flops 1610612736 | bytes 6291456 | tf_op jit(solution)/shard_map/rotated_grad/pallas_call | solution.py:171
  73.9 4.0 %rotated_grad.7 = (bf16[128,1536]{1,0:T(8,128)(2,1)S(1)}, bf16[128,1536]{1,0:T(8,128)(2,1)S(1)}) custom-call(bf16[256,2048]{1,0:T(8,128)(2,1)S(1)} %pad_maximum_fusion.1.grads_ref.refs_4_, bf16[7168,2048]{1,0:T(8,128)(2,1)} %weight_ref.15), custom_call_target="tpu_custom_call" | custom-call | flops 1610612736 | bytes 6291456 | tf_op jit(solution)/shard_map/rotated_grad/pallas_call | solution.py:171
  82.2 2.2 collective-permute-start.13
  84.5 4.8 %rotated_grad.6 = (bf16[128,2048]{1,0:T(8,128)(2,1)S(1)}, bf16[128,2048]{1,0:T(8,128)(2,1)S(1)}) custom-call(bf16[256,2048]{1,0:T(8,128)(2,1)S(1)} %pad_maximum_fusion.1.grads_ref.refs_4_, bf16[7168,2048]{1,0:T(8,128)(2,1)} %weight_ref.15), custom_call_target="tpu_custom_call" | custom-call | flops 2147483648 | bytes 8388608 | tf_op jit(solution)/shard_map/rotated_grad/pallas_call | solution.py:171
  92.4 12.0 %collective-permute-done.12.received_ref = bf16[128,2048]{1,0:T(8,128)(2,1)S(1)} collective-permute-done((bf16[128,2048]{1,0:T(8,128)(2,1)S(1)}, bf16[128,2048]{1,0:T(8,128)(2,1)S(1)}, u32[]{:S(2)}, u32[]{:S(2)}) %collective-permute-start.12) | collective-permute-done | bytes 524320 | tf_op jit(solution)/shard_map/ppermute | solution.py:18
  109.2 6.5 %collective-permute-done.9.received_ref = bf16[128,2048]{1,0:T(8,128)(2,1)S(1)} collective-permute-done((bf16[128,2048]{1,0:T(8,128)(2,1)S(1)}, bf16[128,2048]{1,0:T(8,128)(2,1)S(1)}, u32[]{:S(2)}, u32[]{:S(2)}) %collective-permute-start.9) | collective-permute-done | bytes 524320 | tf_op jit(solution)/shard_map/ppermute | solution.py:18
  116.9 2.3 collective-permute-done.14
  120.8 6.8 %collective-permute-done.15.received_ref = bf16[128,1536]{1,0:T(8,128)(2,1)S(1)} collective-permute-done((bf16[128,1536]{1,0:T(8,128)(2,1)S(1)}, bf16[128,1536]{1,0:T(8,128)(2,1)S(1)}, u32[]{:S(2)}, u32[]{:S(2)}) %collective-permute-start.15) | collective-permute-done | bytes 393248 | tf_op jit(solution)/shard_map/ppermute | solution.py:18
  127.6 7.3 %collective-permute-start.26 = (bf16[2048,256]{1,0:T(8,128)(2,1)S(1)}, bf16[2048,256]{1,0:T(8,128)(2,1)S(1)}, u32[]{:S(2)}, u32[]{:S(2)}) collective-permute-start(bf16[2048,256]{1,0:T(8,128)(2,1)S(1)} %constant_dynamic-update-slice_fusion.2.turned_ref.refs_0_), channel_id=1, source_target_pairs={{0,16},{8,24},{16,0},{24,8},{1,17},{9,25},{17,1},{25,9},{2,18},{10... | collective-permute-start | bytes 3145736 | tf_op jit(solution)/shard_map/ppermute | solution.py:18
  135.0 5.1 %output.4.refs_0_ = f32[256,2048]{1,0:T(8,128)S(1)} custom-call(bf16[2048,256]{1,0:T(8,128)(2,1)S(1)} %constant_dynamic-update-slice_fusion.2.turned_ref.refs_0_, bf16[7168,2048]{1,0:T(8,128)(2,1)} %weight_ref.15), custom_call_target="tpu_custom_call" | custom-call | flops 2147483648 | bytes 8388608 | tf_op jit(solution)/shard_map/output/pallas_call | solution.py:220
  142.5 5.3 %output.5.refs_0_ = f32[256,2048]{1,0:T(8,128)S(1)} custom-call(bf16[2048,256]{1,0:T(8,128)(2,1)} %constant_dynamic-update-slice_fusion.4.turned_ref.refs_0_, bf16[7168,2048]{1,0:T(8,128)(2,1)} %weight_ref.15, f32[256,2048]{1,0:T(8,128)S(1)} %output.4.refs_0_), custom_call_target="tpu_custom_call" | custom-call | flops 2147483648 | bytes 8388608 | tf_op jit(solution)/shard_map/output/pallas_call | solution.py:220
  152.4 4.1 %collective-permute-done.26.refs_1_ = bf16[2048,256]{1,0:T(8,128)(2,1)S(1)} collective-permute-done((bf16[2048,256]{1,0:T(8,128)(2,1)S(1)}, bf16[2048,256]{1,0:T(8,128)(2,1)S(1)}, u32[]{:S(2)}, u32[]{:S(2)}) %collective-permute-start.26) | collective-permute-done | bytes 1048608 | tf_op jit(solution)/shard_map/ppermute | solution.py:18
  157.2 3.2 %collective-permute-done.20 = bf16[1536,128]{1,0:T(8,128)(2,1)S(1)} collective-permute-done((bf16[1536,128]{1,0:T(8,128)(2,1)S(1)}, bf16[1536,128]{1,0:T(8,128)(2,1)S(1)}, u32[]{:S(2)}, u32[]{:S(2)}) %collective-permute-start.20) | collective-permute-done | bytes 393248 | tf_op jit(solution)/shard_map/ppermute | solution.py:18
  162.4 5.7 %collective-permute-start.32 = (bf16[1536,256]{1,0:T(8,128)(2,1)S(1)}, bf16[1536,256]{1,0:T(8,128)(2,1)}, u32[]{:S(2)}, u32[]{:S(2)}) collective-permute-start(bf16[1536,256]{1,0:T(8,128)(2,1)S(1)} %constant_dynamic-update-slice_fusion.6.turned_ref.refs_0_), channel_id=1, source_target_pairs={{0,16},{8,24},{16,0},{24,8},{1,17},{9,25},{17,1},{25,9},{2,18},{10... | collective-permute-start | bytes 2359304 | tf_op jit(solution)/shard_map/ppermute | solution.py:18
  168.9 2.3 collective-permute-start.30
  173.9 7.4 %collective-permute-start.35 = (bf16[1536,256]{1,0:T(8,128)(2,1)}, bf16[1536,256]{1,0:T(8,128)(2,1)}, u32[]{:S(2)}, u32[]{:S(2)}) collective-permute-start(bf16[1536,256]{1,0:T(8,128)(2,1)} %constant_dynamic-update-slice_fusion.8.turned_ref.refs_0_), channel_id=1, source_target_pairs={{0,16},{8,24},{16,0},{24,8},{1,17},{9,25},{17,1},{25,9},{2,18},{10... | collective-permute-start | bytes 2359304 | tf_op jit(solution)/shard_map/ppermute | solution.py:18
  181.4 4.2 %output.6.refs_0_ = f32[256,2048]{1,0:T(8,128)S(1)} custom-call(bf16[1536,256]{1,0:T(8,128)(2,1)S(1)} %constant_dynamic-update-slice_fusion.6.turned_ref.refs_0_, bf16[7168,2048]{1,0:T(8,128)(2,1)} %weight_ref.15, f32[256,2048]{1,0:T(8,128)S(1)} %output.5.refs_0_), custom_call_target="tpu_custom_call" | custom-call | flops 1610612736 | bytes 6291456 | tf_op jit(solution)/shard_map/output/pallas_call | solution.py:220
  185.6 4.3 %output.7 = bf16[256,2048]{1,0:T(8,128)(2,1)S(1)} custom-call(bf16[1536,256]{1,0:T(8,128)(2,1)} %constant_dynamic-update-slice_fusion.8.turned_ref.refs_0_, bf16[7168,2048]{1,0:T(8,128)(2,1)} %weight_ref.15, f32[256,2048]{1,0:T(8,128)S(1)} %output.6.refs_0_), custom_call_target="tpu_custom_call" | custom-call | flops 1610612736 | bytes 6291456 | tf_op jit(solution)/shard_map/output/pallas_call | solution.py:220
  193.1 10.7 %weight_grad.4.refs_8_ = bf16[7168,2048]{1,0:T(8,128)(2,1)} custom-call(bf16[2048,256]{1,0:T(8,128)(2,1)S(1)} %constant_dynamic-update-slice_fusion.2.turned_ref.refs_0_, bf16[2048,256]{1,0:T(8,128)(2,1)S(1)} %collective-permute-done.26.refs_1_, bf16[2048,256]{1,0:T(8,128)(2,1)S(1)} %collective-permute-done.27.refs_2_, ...), custom_call_target="tpu_custom_call" | custom-call | flops 85899344 | bytes 125829 | tf_op jit(solution)/shard_map/weight_grad/pallas_call | solution.py:255
  205.3 6.5 %collective-permute-done.31.received_ref = bf16[128,1536]{1,0:T(8,128)(2,1)S(1)} collective-permute-done((bf16[128,1536]{1,0:T(8,128)(2,1)S(1)}, bf16[128,1536]{1,0:T(8,128)(2,1)S(1)}, u32[]{:S(2)}, u32[]{:S(2)}) %collective-permute-start.31) | collective-permute-done | bytes 393248 | tf_op jit(solution)/shard_map/ppermute | solution.py:18
  214.7 2.7 %collective-permute-start.24 = (bf16[128,2048]{1,0:T(8,128)(2,1)}, bf16[128,2048]{1,0:T(8,128)(2,1)}, u32[]{:S(2)}, u32[]{:S(2)}) collective-permute-start(bf16[128,2048]{1,0:T(8,128)(2,1)} %pad_maximum_fusion.2), channel_id=1, source_target_pairs={{0,1},{1,0},{2,3},{3,2},{4,5},{5,4},{6,7},{7,6},{8,9},{9,8},{10,11... | collective-permute-start | bytes 1572872 | tf_op jit(solution)/shard_map/ppermute | solution.py:18
  218.6 9.5 %weight_grad.5.refs_8_ = bf16[7168,2048]{1,0:T(8,128)(2,1)} custom-call(bf16[1536,256]{1,0:T(8,128)(2,1)S(1)} %constant_dynamic-update-slice_fusion.6.turned_ref.refs_0_, bf16[1536,256]{1,0:T(8,128)(2,1)} %collective-permute-done.32.refs_1_, bf16[1536,256]{1,0:T(8,128)(2,1)} %collective-permute-done.33.refs_2_, ...), custom_call_target="tpu_custom_call", output_to_operand_aliasing={{}: (8, {})} | custom-call | flops 64424508 | bytes 94371 | tf_op jit(solution)/shard_map/weight_grad/pallas_call | solution.py:255
  228.1 9.7 %weight_grad.6.refs_8_ = bf16[7168,2048]{1,0:T(8,128)(2,1)} custom-call(bf16[1536,256]{1,0:T(8,128)(2,1)} %constant_dynamic-update-slice_fusion.8.turned_ref.refs_0_, bf16[1536,256]{1,0:T(8,128)(2,1)} %collective-permute-done.35.refs_1_, bf16[1536,256]{1,0:T(8,128)(2,1)} %collective-permute-done.36.refs_2_, ...), custom_call_target="tpu_custom_call", output_to_operand_aliasing={{}: (8, {})} | custom-call | flops 64424508 | bytes 94371 | tf_op jit(solution)/shard_map/weight_grad/pallas_call | solution.py:255
  240.2 2.4 finish_grad.7
  244.0 12.0 %weight_grad.7 = bf16[7168,2048]{1,0:T(8,128)(2,1)} custom-call(bf16[2048,256]{1,0:T(8,128)(2,1)} %constant_dynamic-update-slice_fusion.4.turned_ref.refs_0_, bf16[2048,256]{1,0:T(8,128)(2,1)} %collective-permute-done.40.refs_1_, bf16[2048,256]{1,0:T(8,128)(2,1)} %collective-permute-done.41.refs_2_, ...), custom_call_target="tpu_custom_call", output_to_operand_aliasing={{}: (8, {})} | custom-call | flops 85899344 | bytes 125829 | tf_op jit(solution)/shard_map/weight_grad/pallas_call | solution.py:255
  (147 shorter events, 57.9 us)
Async XLA Ops:
  16.9 23.0 %collective-permute-start.1 = (bf16[128,2048]{1,0:T(8,128)(2,1)S(1)}, bf16[128,2048]{1,0:T(8,128)(2,1)S(1)}, u32[]{:S(2)}, u32[]{:S(2)}) collective-permute-start(bf16[128,2048]{1,0:T(8,128)(2,1)S(1)} %constant_dynamic-update-slice_fusion), channel_id=1, source_target_pairs={{0,1},{1,0},{2,3},{3,2},{4,5},{5,4},{6,7},{7,6},{8,9},{9,8},{10,11... | collective-permute-start | bytes 1572872 | tf_op jit(solution)/shard_map/ppermute | solution.py:18
  18.9 34.8 %collective-permute-start.2 = (bf16[128,2048]{1,0:T(8,128)(2,1)S(1)}, bf16[128,2048]{1,0:T(8,128)(2,1)S(1)}, u32[]{:S(2)}, u32[]{:S(2)}) collective-permute-start(bf16[128,2048]{1,0:T(8,128)(2,1)S(1)} %slice.19.own_ref), channel_id=1, source_target_pairs={{0,2},{1,3},{2,0},{3,1},{4,6},{5,7},{6,4},{7,5},{8,10},{9,11},{10,... | collective-permute-start | bytes 1572872 | tf_op jit(solution)/shard_map/ppermute | solution.py:18
  40.3 37.7 %collective-permute-start.4 = (bf16[256,2048]{1,0:T(8,128)(2,1)S(1)}, bf16[256,2048]{1,0:T(8,128)(2,1)S(1)}, u32[]{:S(2)}, u32[]{:S(2)}) collective-permute-start(bf16[256,2048]{1,0:T(8,128)(2,1)S(1)} %pad_maximum_fusion.1.grads_ref.refs_4_), channel_id=1, source_target_pairs={{0,16},{8,24},{16,0},{24,8},{1,17},{9,25},{17,1},{25,9},{2,18},{10... | collective-permute-start | bytes 3145736 | tf_op jit(solution)/shard_map/ppermute | solution.py:18
  42.7 29.5 %collective-permute-start.3 = (bf16[128,1536]{1,0:T(8,128)(2,1)S(1)}, bf16[128,1536]{1,0:T(8,128)(2,1)}, u32[]{:S(2)}, u32[]{:S(2)}) collective-permute-start(bf16[128,1536]{1,0:T(8,128)(2,1)S(1)} %slice.18.own_ref), channel_id=1, source_target_pairs={{0,2},{1,3},{2,0},{3,1},{4,6},{5,7},{6,4},{7,5},{8,10},{9,11},{10,... | collective-permute-start | bytes 1179656 | tf_op jit(solution)/shard_map/ppermute | solution.py:18
  55.7 22.3 %collective-permute-start.10 = (bf16[128,2048]{1,0:T(8,128)(2,1)S(1)}, bf16[128,2048]{1,0:T(8,128)(2,1)}, u32[]{:S(2)}, u32[]{:S(2)}) collective-permute-start(bf16[128,2048]{1,0:T(8,128)(2,1)S(1)} %combine.12.own_ref), channel_id=1, source_target_pairs={{0,1},{1,0},{2,3},{3,2},{4,5},{5,4},{6,7},{7,6},{8,9},{9,8},{10,11... | collective-permute-start | bytes 1572872 | tf_op jit(solution)/shard_map/ppermute | solution.py:18
  62.1 17.7 %collective-permute-start.11 = (bf16[128,2048]{1,0:T(8,128)(2,1)}, bf16[128,2048]{1,0:T(8,128)(2,1)}, u32[]{:S(2)}, u32[]{:S(2)}) collective-permute-start(bf16[128,2048]{1,0:T(8,128)(2,1)} %get-tuple-element.118), channel_id=1, source_target_pairs={{0,4},{4,0},{1,5},{5,1},{2,6},{6,2},{3,7},{7,3},{8,12},{12,8},{9,1... | collective-permute-start | bytes 1572872 | tf_op jit(solution)/shard_map/ppermute | solution.py:18
  65.5 25.5 %collective-permute-start.6 = (bf16[128,2048]{1,0:T(8,128)(2,1)}, bf16[128,2048]{1,0:T(8,128)(2,1)}, u32[]{:S(2)}, u32[]{:S(2)}) collective-permute-start(bf16[128,2048]{1,0:T(8,128)(2,1)} %slice.20.own_ref), channel_id=1, source_target_pairs={{0,2},{1,3},{2,0},{3,1},{4,6},{5,7},{6,4},{7,5},{8,10},{9,11},{10,... | collective-permute-start | bytes 1572872 | tf_op jit(solution)/shard_map/ppermute | solution.py:18
  77.9 28.9 %collective-permute-start.7 = (bf16[256,2048]{1,0:T(8,128)(2,1)S(1)}, bf16[256,2048]{1,0:T(8,128)(2,1)S(1)}, u32[]{:S(2)}, u32[]{:S(2)}) collective-permute-start(bf16[256,2048]{1,0:T(8,128)(2,1)S(1)} %collective-permute-done.4.refs_5_), channel_id=1, source_target_pairs={{0,8},{8,0},{16,24},{24,16},{1,9},{9,1},{17,25},{25,17},{2,10},{10... | collective-permute-start | bytes 3145736 | tf_op jit(solution)/shard_map/ppermute | solution.py:18
  81.1 23.3 %collective-permute-start.12 = (bf16[128,2048]{1,0:T(8,128)(2,1)S(1)}, bf16[128,2048]{1,0:T(8,128)(2,1)S(1)}, u32[]{:S(2)}, u32[]{:S(2)}) collective-permute-start(bf16[128,2048]{1,0:T(8,128)(2,1)S(1)} %combine.17.own_ref), channel_id=1, source_target_pairs={{0,1},{1,0},{2,3},{3,2},{4,5},{5,4},{6,7},{7,6},{8,9},{9,8},{10,11... | collective-permute-start | bytes 1572872 | tf_op jit(solution)/shard_map/ppermute | solution.py:18
  82.2 23.9 %collective-permute-start.13 = (bf16[128,1536]{1,0:T(8,128)(2,1)S(1)}, bf16[128,1536]{1,0:T(8,128)(2,1)S(1)}, u32[]{:S(2)}, u32[]{:S(2)}) collective-permute-start(bf16[128,1536]{1,0:T(8,128)(2,1)S(1)} %slice.21.own_ref), channel_id=1, source_target_pairs={{0,2},{1,3},{2,0},{3,1},{4,6},{5,7},{6,4},{7,5},{8,10},{9,11},{10,... | collective-permute-start | bytes 1179656 | tf_op jit(solution)/shard_map/ppermute | solution.py:18
  89.4 17.6 %collective-permute-start.8 = (bf16[128,2048]{1,0:T(8,128)(2,1)S(1)}, bf16[128,2048]{1,0:T(8,128)(2,1)S(1)}, u32[]{:S(2)}, u32[]{:S(2)}) collective-permute-start(bf16[128,2048]{1,0:T(8,128)(2,1)S(1)} %get-tuple-element.108), channel_id=1, source_target_pairs={{0,4},{4,0},{1,5},{5,1},{2,6},{6,2},{3,7},{7,3},{8,12},{12,8},{9,1... | collective-permute-start | bytes 1572872 | tf_op jit(solution)/shard_map/ppermute | solution.py:18
  92.3 23.3 %collective-permute-start.9 = (bf16[128,2048]{1,0:T(8,128)(2,1)S(1)}, bf16[128,2048]{1,0:T(8,128)(2,1)S(1)}, u32[]{:S(2)}, u32[]{:S(2)}) collective-permute-start(bf16[128,2048]{1,0:T(8,128)(2,1)S(1)} %combine.15.own_ref), channel_id=1, source_target_pairs={{0,1},{1,0},{2,3},{3,2},{4,5},{5,4},{6,7},{7,6},{8,9},{9,8},{10,11... | collective-permute-start | bytes 1572872 | tf_op jit(solution)/shard_map/ppermute | solution.py:18
  106.1 21.5 %collective-permute-start.15 = (bf16[128,1536]{1,0:T(8,128)(2,1)S(1)}, bf16[128,1536]{1,0:T(8,128)(2,1)S(1)}, u32[]{:S(2)}, u32[]{:S(2)}) collective-permute-start(bf16[128,1536]{1,0:T(8,128)(2,1)S(1)} %get-tuple-element.127), channel_id=1, source_target_pairs={{0,4},{4,0},{1,5},{5,1},{2,6},{6,2},{3,7},{7,3},{8,12},{12,8},{9,1... | collective-permute-start | bytes 1179656 | tf_op jit(solution)/shard_map/ppermute | solution.py:18
  106.9 35.0 %collective-permute-start.17 = (bf16[128,1536]{1,0:T(8,128)(2,1)S(1)}, bf16[128,1536]{1,0:T(8,128)(2,1)S(1)}, u32[]{:S(2)}, u32[]{:S(2)}) collective-permute-start(bf16[128,1536]{1,0:T(8,128)(2,1)S(1)} %combine.13.own_ref), channel_id=1, source_target_pairs={{0,1},{1,0},{2,3},{3,2},{4,5},{5,4},{6,7},{7,6},{8,9},{9,8},{10,11... | collective-permute-start | bytes 1179656 | tf_op jit(solution)/shard_map/ppermute | solution.py:18
  107.0 40.8 %collective-permute-start.18 = (bf16[128,1536]{1,0:T(8,128)(2,1)S(1)}, bf16[128,1536]{1,0:T(8,128)(2,1)S(1)}, u32[]{:S(2)}, u32[]{:S(2)}) collective-permute-start(bf16[128,1536]{1,0:T(8,128)(2,1)S(1)} %combine.19.own_ref), channel_id=1, source_target_pairs={{0,1},{1,0},{2,3},{3,2},{4,5},{5,4},{6,7},{7,6},{8,9},{9,8},{10,11... | collective-permute-start | bytes 1179656 | tf_op jit(solution)/shard_map/ppermute | solution.py:18
  115.6 33.3 %collective-permute-start.19 = (bf16[128,2048]{1,0:T(8,128)(2,1)S(1)}, bf16[128,2048]{1,0:T(8,128)(2,1)S(1)}, u32[]{:S(2)}, u32[]{:S(2)}) collective-permute-start(bf16[128,2048]{1,0:T(8,128)(2,1)S(1)} %combine.18.own_ref), channel_id=1, source_target_pairs={{0,2},{1,3},{2,0},{3,1},{4,6},{5,7},{6,4},{7,5},{8,10},{9,11},{10,... | collective-permute-start | bytes 1572872 | tf_op jit(solution)/shard_map/ppermute | solution.py:18
  119.2 21.8 %collective-permute-start.16 = (bf16[2048,128]{1,0:T(8,128)(2,1)S(1)}, bf16[2048,128]{1,0:T(8,128)(2,1)S(1)}, u32[]{:S(2)}, u32[]{:S(2)}) collective-permute-start(bf16[2048,128]{1,0:T(8,128)(2,1)S(1)} %finish_hidden.4), channel_id=1, source_target_pairs={{0,4},{4,0},{1,5},{5,1},{2,6},{6,2},{3,7},{7,3},{8,12},{12,8},{9,1... | collective-permute-start | bytes 1572872 | tf_op jit(solution)/shard_map/ppermute | solution.py:18
  127.6 28.9 %collective-permute-start.26 = (bf16[2048,256]{1,0:T(8,128)(2,1)S(1)}, bf16[2048,256]{1,0:T(8,128)(2,1)S(1)}, u32[]{:S(2)}, u32[]{:S(2)}) collective-permute-start(bf16[2048,256]{1,0:T(8,128)(2,1)S(1)} %constant_dynamic-update-slice_fusion.2.turned_ref.refs_0_), channel_id=1, source_target_pairs={{0,16},{8,24},{16,0},{24,8},{1,17},{9,25},{17,1},{25,9},{2,18},{10... | collective-permute-start | bytes 3145736 | tf_op jit(solution)/shard_map/ppermute | solution.py:18
  141.0 21.4 %collective-permute-start.29 = (bf16[256,2048]{1,0:T(8,128)(2,1)S(1)}, bf16[256,2048]{1,0:T(8,128)(2,1)S(1)}, u32[]{:S(2)}, u32[]{:S(2)}) collective-permute-start(bf16[256,2048]{1,0:T(8,128)(2,1)S(1)} %pad_maximum_fusion.1.grads_ref.refs_4_), channel_id=1, source_target_pairs={{0,8},{8,0},{16,24},{24,16},{1,9},{9,1},{17,25},{25,17},{2,10},{10... | collective-permute-start | bytes 3145736 | tf_op jit(solution)/shard_map/ppermute | solution.py:18
  156.5 17.4 %collective-permute-start.25 = (bf16[128,2048]{1,0:T(8,128)(2,1)S(1)}, bf16[128,2048]{1,0:T(8,128)(2,1)S(1)}, u32[]{:S(2)}, u32[]{:S(2)}) collective-permute-start(bf16[128,2048]{1,0:T(8,128)(2,1)S(1)} %combine.16.own_ref), channel_id=1, source_target_pairs={{0,1},{1,0},{2,3},{3,2},{4,5},{5,4},{6,7},{7,6},{8,9},{9,8},{10,11... | collective-permute-start | bytes 1572872 | tf_op jit(solution)/shard_map/ppermute | solution.py:18
  160.3 31.6 %collective-permute-start.28 = (bf16[2048,256]{1,0:T(8,128)(2,1)S(1)}, bf16[2048,256]{1,0:T(8,128)(2,1)S(1)}, u32[]{:S(2)}, u32[]{:S(2)}) collective-permute-start(bf16[2048,256]{1,0:T(8,128)(2,1)S(1)} %collective-permute-done.26.refs_1_), channel_id=1, source_target_pairs={{0,8},{8,0},{16,24},{24,16},{1,9},{9,1},{17,25},{25,17},{2,10},{10... | collective-permute-start | bytes 3145736 | tf_op jit(solution)/shard_map/ppermute | solution.py:18
  162.2 30.7 %collective-permute-start.27 = (bf16[2048,256]{1,0:T(8,128)(2,1)S(1)}, bf16[2048,256]{1,0:T(8,128)(2,1)S(1)}, u32[]{:S(2)}, u32[]{:S(2)}) collective-permute-start(bf16[2048,256]{1,0:T(8,128)(2,1)S(1)} %constant_dynamic-update-slice_fusion.2.turned_ref.refs_0_), channel_id=1, source_target_pairs={{0,8},{8,0},{16,24},{24,16},{1,9},{9,1},{17,25},{25,17},{2,10},{10... | collective-permute-start | bytes 3145736 | tf_op jit(solution)/shard_map/ppermute | solution.py:18
  162.4 29.6 %collective-permute-start.32 = (bf16[1536,256]{1,0:T(8,128)(2,1)S(1)}, bf16[1536,256]{1,0:T(8,128)(2,1)}, u32[]{:S(2)}, u32[]{:S(2)}) collective-permute-start(bf16[1536,256]{1,0:T(8,128)(2,1)S(1)} %constant_dynamic-update-slice_fusion.6.turned_ref.refs_0_), channel_id=1, source_target_pairs={{0,16},{8,24},{16,0},{24,8},{1,17},{9,25},{17,1},{25,9},{2,18},{10... | collective-permute-start | bytes 2359304 | tf_op jit(solution)/shard_map/ppermute | solution.py:18
  168.9 23.0 %collective-permute-start.30 = (bf16[128,1536]{1,0:T(8,128)(2,1)S(1)}, bf16[128,1536]{1,0:T(8,128)(2,1)S(1)}, u32[]{:S(2)}, u32[]{:S(2)}) collective-permute-start(bf16[128,1536]{1,0:T(8,128)(2,1)S(1)} %combine.22.own_ref), channel_id=1, source_target_pairs={{0,2},{1,3},{2,0},{3,1},{4,6},{5,7},{6,4},{7,5},{8,10},{9,11},{10,... | collective-permute-start | bytes 1179656 | tf_op jit(solution)/shard_map/ppermute | solution.py:18
  173.9 31.0 %collective-permute-start.35 = (bf16[1536,256]{1,0:T(8,128)(2,1)}, bf16[1536,256]{1,0:T(8,128)(2,1)}, u32[]{:S(2)}, u32[]{:S(2)}) collective-permute-start(bf16[1536,256]{1,0:T(8,128)(2,1)} %constant_dynamic-update-slice_fusion.8.turned_ref.refs_0_), channel_id=1, source_target_pairs={{0,16},{8,24},{16,0},{24,8},{1,17},{9,25},{17,1},{25,9},{2,18},{10... | collective-permute-start | bytes 2359304 | tf_op jit(solution)/shard_map/ppermute | solution.py:18
  191.9 21.9 %collective-permute-start.33 = (bf16[1536,256]{1,0:T(8,128)(2,1)S(1)}, bf16[1536,256]{1,0:T(8,128)(2,1)}, u32[]{:S(2)}, u32[]{:S(2)}) collective-permute-start(bf16[1536,256]{1,0:T(8,128)(2,1)S(1)} %constant_dynamic-update-slice_fusion.6.turned_ref.refs_0_), channel_id=1, source_target_pairs={{0,8},{8,0},{16,24},{24,16},{1,9},{9,1},{17,25},{25,17},{2,10},{10... | collective-permute-start | bytes 2359304 | tf_op jit(solution)/shard_map/ppermute | solution.py:18
  191.9 19.9 %collective-permute-start.31 = (bf16[128,1536]{1,0:T(8,128)(2,1)S(1)}, bf16[128,1536]{1,0:T(8,128)(2,1)S(1)}, u32[]{:S(2)}, u32[]{:S(2)}) collective-permute-start(bf16[128,1536]{1,0:T(8,128)(2,1)S(1)} %combine.21.own_ref), channel_id=1, source_target_pairs={{0,2},{1,3},{2,0},{3,1},{4,6},{5,7},{6,4},{7,5},{8,10},{9,11},{10,... | collective-permute-start | bytes 1179656 | tf_op jit(solution)/shard_map/ppermute | solution.py:18
  192.0 45.7 %collective-permute-start.40 = (bf16[2048,256]{1,0:T(8,128)(2,1)}, bf16[2048,256]{1,0:T(8,128)(2,1)}, u32[]{:S(2)}, u32[]{:S(2)}) collective-permute-start(bf16[2048,256]{1,0:T(8,128)(2,1)} %constant_dynamic-update-slice_fusion.4.turned_ref.refs_0_), channel_id=1, source_target_pairs={{0,16},{8,24},{16,0},{24,8},{1,17},{9,25},{17,1},{25,9},{2,18},{10... | collective-permute-start | bytes 3145736 | tf_op jit(solution)/shard_map/ppermute | solution.py:18
  192.9 21.8 %collective-permute-start.34 = (bf16[1536,256]{1,0:T(8,128)(2,1)}, bf16[1536,256]{1,0:T(8,128)(2,1)}, u32[]{:S(2)}, u32[]{:S(2)}) collective-permute-start(bf16[1536,256]{1,0:T(8,128)(2,1)} %collective-permute-done.32.refs_1_), channel_id=1, source_target_pairs={{0,8},{8,0},{16,24},{24,16},{1,9},{9,1},{17,25},{25,17},{2,10},{10... | collective-permute-start | bytes 2359304 | tf_op jit(solution)/shard_map/ppermute | solution.py:18
  204.9 23.1 %collective-permute-start.36 = (bf16[1536,256]{1,0:T(8,128)(2,1)}, bf16[1536,256]{1,0:T(8,128)(2,1)}, u32[]{:S(2)}, u32[]{:S(2)}) collective-permute-start(bf16[1536,256]{1,0:T(8,128)(2,1)} %constant_dynamic-update-slice_fusion.8.turned_ref.refs_0_), channel_id=1, source_target_pairs={{0,8},{8,0},{16,24},{24,16},{1,9},{9,1},{17,25},{25,17},{2,10},{10... | collective-permute-start | bytes 2359304 | tf_op jit(solution)/shard_map/ppermute | solution.py:18
  213.8 26.4 %collective-permute-start.38 = (bf16[128,2048]{1,0:T(8,128)(2,1)}, bf16[128,2048]{1,0:T(8,128)(2,1)}, u32[]{:S(2)}, u32[]{:S(2)}) collective-permute-start(bf16[128,2048]{1,0:T(8,128)(2,1)} %copy-done.9), channel_id=1, source_target_pairs={{0,2},{1,3},{2,0},{3,1},{4,6},{5,7},{6,4},{7,5},{8,10},{9,11},{10,... | collective-permute-start | bytes 1572872 | tf_op jit(solution)/shard_map/ppermute | solution.py:18
  214.7 27.9 %collective-permute-start.24 = (bf16[128,2048]{1,0:T(8,128)(2,1)}, bf16[128,2048]{1,0:T(8,128)(2,1)}, u32[]{:S(2)}, u32[]{:S(2)}) collective-permute-start(bf16[128,2048]{1,0:T(8,128)(2,1)} %pad_maximum_fusion.2), channel_id=1, source_target_pairs={{0,1},{1,0},{2,3},{3,2},{4,5},{5,4},{6,7},{7,6},{8,9},{9,8},{10,11... | collective-permute-start | bytes 1572872 | tf_op jit(solution)/shard_map/ppermute | solution.py:18
  (31 other events, 374.5 us)
